TPU v7x, 32 devices: a whole 2x2x4 slice. The times are simulated.
32 devices in a mesh: tm: 4 (over y, x), space: 8 (over z, core).
Axes of the slice: x: 2, y: 2, z: 4, core: 2. Of those that a mesh axis runs over, the one named last changes fastest.
Arguments:
- starts: float32 [8, 8, 32, 16, 1024], P('tm', None, 'space'), may hold values from 0 to 2
- pore_mask: int32 [32, 16, 1024], P('space'), may hold values 0 or 1
- phase_label: int32 [32, 16, 1024], P('space'), may hold values from 0 to 3
- diffusivity: float32 [8], replicated, may hold values from 0.08 to 0.16
- stoich: float32 [8], replicated, may hold values from -1 to 1
- phase_rate: float32 [4], replicated, may hold values from 0.02 to 0.1
Outputs:
- ends: float32 [8, 8, 32, 16, 1024], P('tm', None, 'space')
Inputs may be any that keep to these rules, and one draw needn't show every extreme that they name: `pore_mask`: 0 marks solid cells, 1 pore cells.
All inputs are finite; a program needn't handle non-finite values. No bound on the sum of `pore_mask` on one device may be relied on, other than what follows from the above.
Results may differ from a plain program's by a relative error of at most 0.00011.
Values sent between devices are 32-bit elements; how exact they have to be, the bound alone decides.
A program may use at most 192 MiB of HBM per device.

v0:
```python
import jax
import jax.numpy as jnp
from jax import lax
from jax.sharding import PartitionSpec as P

PHASES = 4
SUBSTEPS = 4


def extended(block, sides, width):
    for axis, dim in sides:
        count = lax.axis_size(axis)
        forward = [(i, i + 1) for i in range(count - 1)]
        forward.append((count - 1, 0))
        backward = [(target, source) for source, target in forward]
        low = lax.ppermute(
            lax.slice_in_dim(block, block.shape[dim] - width, None, axis=dim), axis, forward
        )
        high = lax.ppermute(lax.slice_in_dim(block, 0, width, axis=dim), axis, backward)
        block = jnp.concatenate([low, block, high], axis=dim)
    return block


def shifted_2(value, axis, steps):
    count = lax.axis_size(axis)
    first, last = (max(0, -steps), min(count, count - steps))
    return lax.ppermute(value, axis, [(source, source + steps) for source in range(first, last)])


def shifted(array, axis, step):
    count = array.shape[axis]
    widths = [(0, 0)] * array.ndim
    if step > 0:
        widths[axis] = (0, step)
        return lax.slice_in_dim(jnp.pad(array, widths), step, step + count, axis=axis)
    widths[axis] = (-step, 0)
    return lax.slice_in_dim(jnp.pad(array, widths), 0, count, axis=axis)


def explicit_step(padded, weight_wide, source, coef, rscale, stoich):
    conc = padded[..., 1:-1, :, :]
    weight = weight_wide[1:-1]
    total = weight_wide[2:] * (padded[..., 2:, :, :] - conc) + weight_wide[:-2] * (
        padded[..., :-2, :, :] - conc
    )
    for axis in (1, 2):
        for step in (1, -1):
            total = total + shifted(weight, axis, step) * (
                shifted(conc, conc.ndim - 3 + axis, step) - conc
            )
    diffusion = coef[:, None, None, None] * (weight * total)
    rate = source * (1.0 - conc[..., 0, :, :, :] * conc[..., 1, :, :, :])
    return conc + diffusion + rscale * stoich[:, None, None, None] * rate[..., None, :, :, :]


def pair_table(length):
    rows = lax.broadcasted_iota(jnp.int32, (length, length // 2), 0)
    cols = lax.broadcasted_iota(jnp.int32, (length, length // 2), 1)
    return jnp.where(rows // 2 == cols, jnp.float32(1.0), jnp.float32(0.0))


def restrict(array):
    summed = array[..., 0::2, :, :] + array[..., 1::2, :, :]
    summed = summed[..., 0::2, :] + summed[..., 1::2, :]
    table = pair_table(array.shape[-1])
    folded = jnp.einsum("...z,zw->...w", summed, table, precision=lax.Precision.HIGHEST)
    return folded * jnp.float32(0.125)


def prolong(array):
    table = pair_table(2 * array.shape[-1])
    spread = jnp.einsum("...w,zw->...z", array, table, precision=lax.Precision.HIGHEST)
    shape = spread.shape
    lead = shape[:-3]
    grown = jnp.broadcast_to(
        spread[..., :, None, :, None, :], lead + (shape[-3], 2, shape[-2], 2, shape[-1])
    )
    return grown.reshape(lead + (2 * shape[-3], 2 * shape[-2], shape[-1]))


def local(starts, pore_mask, phase_label, diffusivity, stoich, phase_rate):
    tile = starts.shape[2]
    local_count = starts.shape[0]
    pores = pore_mask.astype(jnp.float32)
    kappa = jnp.zeros(pores.shape, jnp.float32)
    for phase in range(PHASES):
        kappa = kappa + jnp.where(phase_label == phase, phase_rate[phase], jnp.float32(0.0))
    source = pores * kappa
    margin = 2
    stacked = extended(jnp.stack([pores, source]), (("space", 1),), margin)
    pores_wide = stacked[0]
    porosity_wide = restrict(pores_wide)
    coarse_source = restrict(source)
    coarse_coef = diffusivity * (SUBSTEPS / 4.0)

    def coarse_step(state):
        padded = extended(state, (("space", 2),), 1)
        return explicit_step(
            padded, porosity_wide, coarse_source, coarse_coef, float(SUBSTEPS), stoich
        )

    narrow_pores = pores_wide[1 : tile + 3]
    fines = starts
    for turn in range(SUBSTEPS):
        padded = extended(fines, (("space", 2),), 1)
        fines = explicit_step(padded, narrow_pores, source, diffusivity, 1.0, stoich)
    previous = coarse_step(restrict(starts))
    device_place = lax.axis_index("tm")
    first_state = restrict(starts[0])
    sections = lax.axis_size("tm")
    incoming = jnp.zeros_like(starts[0])
    advanced_all = []
    for section in range(sections):
        carried = jnp.where(device_place == 0, first_state, restrict(incoming))
        advanced_all = []
        finished = None
        for which in range(local_count):
            advanced = coarse_step(carried[None])[0]
            advanced_all.append(advanced)
            finished = prolong(advanced - previous[which]) + fines[which]
            carried = restrict(finished)
        if section + 1 < sections:
            incoming = shifted_2(finished, "tm", 1)
    results = []
    for which in range(local_count):
        results.append(prolong(advanced_all[which] - previous[which]) + fines[which])
    return jnp.stack(results)


def solution(mesh):
    placed = (
        P("tm", None, "space", None, None),
        P("space", None, None),
        P("space", None, None),
        P(),
        P(),
        P(),
    )
    return jax.shard_map(
        local,
        mesh=mesh,
        in_specs=placed,
        out_specs=P("tm", None, "space", None, None),
        check_vma=False,
    )
```

profile of v0, /device:TPU:4, one launch (start us, length us, event | category | flops | bytes accessed | tf_op | source)
XLA Modules:
  0.0 473.2 jit_solution(10200079420353819851)
XLA Ops:
  2.5 3.7 add_multiply_fusion
  7.0 3.5 collective-permute-start.1
  10.5 2.6 slice_add_fusion
  13.2 5.2 %slice.771 = f32[2,8,2,8,1024]{4,3,2,1,0:T(8,128)} slice(f32[2,8,2,16,1024]{4,3,2,1,0:T(8,128)S(1)} %slice_add_fusion), slice={[0:2:1], [0:8:1], [0:2:1], [1:16:2], [0:1024:1]} | slice | bytes 2097152 | tf_op jit(solution)/shard_map/slice | solution.py:64
  18.3 5.2 %slice.770 = f32[2,8,2,8,1024]{4,3,2,1,0:T(8,128)} slice(f32[2,8,2,16,1024]{4,3,2,1,0:T(8,128)S(1)} %slice_add_fusion), slice={[0:2:1], [0:8:1], [0:2:1], [0:16:2], [0:1024:1]} | slice | bytes 2097152 | tf_op jit(solution)/shard_map/slice | solution.py:64
  23.5 4.1 fusion.104
  38.3 17.3 %collective-permute-done.6 = f32[2,8,1,16,1024]{4,3,2,1,0:T(8,128)} collective-permute-done((f32[2,8,1,16,1024]{4,3,2,1,0:T(8,128)}, f32[2,8,1,16,1024]{4,3,2,1,0:T(8,128)}, u32[]{:S(2)}, u32[]{:S(2)}) %collective-permute-start.6) | collective-permute-done | bytes 1048608 | tf_op jit(solution)/shard_map/ppermute | solution.py:19
  57.4 6.6 %fusion.7 = f32[2,8,4,16,1024]{4,3,2,1,0:T(8,128)S(1)} fusion(f32[2,8,4,16,1024]{4,3,2,1,0:T(8,128)S(1)} %copy-done.2, f32[2,8,1,16,1024]{4,3,2,1,0:T(8,128)} %collective-permute-done.7, f32[2,8,1,16,1024]{4,3,2,1,0:T(8,128)} %collective-permute-done.6, f32[2,4,16,1024]{3,2,1,0:T(8,128)S(1)} %multiply_bitcast_fusion, f32[8]{0:T(128)S(1)} %copy-done.56, ...), kind=kLoop, calls=%fused_computation.23 | loop fusion | flops 25165824 | bytes 12845120 | tf_op jit(solution)/shard_map/add | solution.py:53
  69.4 3.7 collective-permute-start.2
  73.2 3.0 fusion.644
  77.5 12.9 %collective-permute-done.8 = f32[2,8,1,16,1024]{4,3,2,1,0:T(8,128)} collective-permute-done((f32[2,8,1,16,1024]{4,3,2,1,0:T(8,128)}, f32[2,8,1,16,1024]{4,3,2,1,0:T(8,128)}, u32[]{:S(2)}, u32[]{:S(2)}) %collective-permute-start.8) | collective-permute-done | bytes 1048608 | tf_op jit(solution)/shard_map/ppermute | solution.py:19
  90.4 3.9 collective-permute-done.9
  94.3 6.6 %fusion.17 = f32[2,8,4,16,1024]{4,3,2,1,0:T(8,128)S(1)} fusion(f32[2,8,4,16,1024]{4,3,2,1,0:T(8,128)S(1)} %copy-done.5, f32[2,8,1,16,1024]{4,3,2,1,0:T(8,128)} %collective-permute-done.9, f32[2,8,1,16,1024]{4,3,2,1,0:T(8,128)} %collective-permute-done.8, f32[2,4,16,1024]{3,2,1,0:T(8,128)S(1)} %fusion.253, f32[8]{0:T(128)S(1)} %copy-done.56, ...), kind=kLoop, calls=%fused_computation.33 | loop fusion | flops 25165824 | bytes 12845120 | tf_op jit(solution)/shard_map/add | solution.py:53
  108.8 18.4 %collective-permute-done.10 = f32[2,8,1,16,1024]{4,3,2,1,0:T(8,128)} collective-permute-done((f32[2,8,1,16,1024]{4,3,2,1,0:T(8,128)}, f32[2,8,1,16,1024]{4,3,2,1,0:T(8,128)}, u32[]{:S(2)}, u32[]{:S(2)}) %collective-permute-start.10) | collective-permute-done | bytes 1048608 | tf_op jit(solution)/shard_map/ppermute | solution.py:19
  127.3 6.6 %fusion.27 = f32[2,8,4,16,1024]{4,3,2,1,0:T(8,128)S(1)} fusion(f32[2,8,4,16,1024]{4,3,2,1,0:T(8,128)S(1)} %copy-done.7, f32[2,8,1,16,1024]{4,3,2,1,0:T(8,128)} %collective-permute-done.11, f32[2,8,1,16,1024]{4,3,2,1,0:T(8,128)} %collective-permute-done.10, f32[2,4,16,1024]{3,2,1,0:T(8,128)S(1)} %fusion.250, f32[8]{0:T(128)S(1)} %copy-done.56, ...), kind=kLoop, calls=%fused_computation.43 | loop fusion | flops 25165824 | bytes 12845120 | tf_op jit(solution)/shard_map/add | solution.py:53
  136.6 3.7 collective-permute-start.12
  142.4 15.7 %collective-permute-done.3 = f32[1,8,1,8,512]{4,3,2,1,0:T(8,128)S(1)} collective-permute-done((f32[1,8,1,8,512]{4,3,2,1,0:T(8,128)S(1)}, f32[1,8,1,8,512]{4,3,2,1,0:T(8,128)S(1)}, u32[]{:S(2)}, u32[]{:S(2)}) %collective-permute-start.3) | collective-permute-done | bytes 131104 | tf_op jit(solution)/shard_map/ppermute | solution.py:16
  158.0 3.7 fusion.98
  164.1 2.7 reshape.231
  168.1 15.2 %fusion.37 = f32[2,8,4,16,1024]{4,3,2,1,0:T(8,128)S(1)} fusion(f32[2,8,4,16,1024]{4,3,2,1,0:T(8,128)} %copy-done.3, f32[2,8,1,16,1024]{4,3,2,1,0:T(8,128)} %collective-permute-done.13, f32[2,8,1,16,1024]{4,3,2,1,0:T(8,128)} %collective-permute-done.12, f32[2,4,16,1024]{3,2,1,0:T(8,128)S(1)} %fusion.247, f32[8]{0:T(128)S(1)} %copy-done.56, ...), kind=kLoop, calls=%fused_computation.53 | loop fusion | flops 25165824 | bytes 12845120 | tf_op jit(solution)/shard_map/add | solution.py:53
  187.8 5.5 %collective-permute-start.15 = (f32[1,8,1,8,512]{4,3,2,1,0:T(8,128)S(1)}, f32[1,8,1,8,512]{4,3,2,1,0:T(8,128)S(1)}, u32[]{:S(2)}, u32[]{:S(2)}) collective-permute-start(f32[1,8,1,8,512]{4,3,2,1,0:T(8,128)S(1)} %get-tuple-element.34), channel_id=1, source_target_pairs={{0,1},{1,2},{2,3},{3,4},{4,5},{5,6},{6,7},{7,0},{8,9},{9,10},{10,1... | collective-permute-start | bytes 393224 | tf_op jit(solution)/shard_map/ppermute | solution.py:16
  194.6 2.8 fusion.96
  199.7 2.7 reshape.232
  204.4 3.5 collective-permute-start.16
  207.9 45.3 %collective-permute-done.16 = f32[8,4,16,1024]{3,2,1,0:T(8,128)S(1)} collective-permute-done((f32[8,4,16,1024]{3,2,1,0:T(8,128)S(1)}, f32[8,4,16,1024]{3,2,1,0:T(8,128)S(1)}, u32[]{:S(2)}, u32[]{:S(2)}) %collective-permute-start.16) | collective-permute-done | bytes 2097184 | tf_op jit(solution)/shard_map/ppermute | solution.py:27
  259.0 3.3 collective-permute-done.18
  262.3 2.8 fusion.94
  267.4 2.7 reshape.233
  277.1 3.9 collective-permute-done.20
  281.0 2.8 fusion.92
  286.1 2.7 reshape.234
  290.8 2.8 collective-permute-start.21
  293.7 48.5 %collective-permute-done.21 = f32[8,4,16,1024]{3,2,1,0:T(8,128)S(1)} collective-permute-done((f32[8,4,16,1024]{3,2,1,0:T(8,128)S(1)}, f32[8,4,16,1024]{3,2,1,0:T(8,128)S(1)}, u32[]{:S(2)}, u32[]{:S(2)}) %collective-permute-start.21) | collective-permute-done | bytes 2097184 | tf_op jit(solution)/shard_map/ppermute | solution.py:27
  347.5 3.5 collective-permute-done.23
  351.0 2.8 fusion.90
  356.1 2.7 reshape.235
  363.7 3.2 collective-permute-done.24
  366.9 2.7 collective-permute-done.25
  369.7 2.8 fusion.88
  374.8 2.7 reshape.236
  377.5 3.3 bitcast_add_fusion
  383.0 45.4 %collective-permute-done.26 = f32[8,4,16,1024]{3,2,1,0:T(8,128)S(1)} collective-permute-done((f32[8,4,16,1024]{3,2,1,0:T(8,128)}, f32[8,4,16,1024]{3,2,1,0:T(8,128)S(1)}, u32[]{:S(2)}, u32[]{:S(2)}) %collective-permute-start.26) | collective-permute-done | bytes 2097184 | tf_op jit(solution)/shard_map/ppermute | solution.py:27
  435.6 3.7 collective-permute-done.28
  439.3 2.8 fusion.86
  453.9 3.0 collective-permute-done.29
  456.9 2.7 collective-permute-done.30
  459.6 2.8 fusion.84
  465.8 6.8 %slice_add_fusion.2 = (f32[2,8,4,16,1024]{4,3,2,1,0:T(8,128)}, f32[2,8,4,16,1024]{4,3,2,1,0:T(8,128)}) fusion(f32[1,8,4,16,1024]{4,3,2,1,0:T(8,128)} %reshape.237, f32[2,8,4,16,1024]{4,3,2,1,0:T(8,128)} %copy-done, f32[1,8,4,16,1024]{4,3,2,1,0:T(8,128)} %reshape.239, f32[2,8,4,16,1024]{4,3,2,1,0:T(8,128)} %custom-call), kind=kLoop, output_to_operand_aliasing={{0}: (3, {}), {1}: (3, {})}, calls=%fused_computation.143 | loop fusion | flops 1048576 | bytes 12582912 | tf_op jit(solution)/shard_map/add | solution.py:126
  (280 shorter events, 106.2 us)
Async XLA Ops:
  6.9 29.9 %collective-permute-start = (f32[2,2,16,1024]{3,2,1,0:T(8,128)}, f32[2,2,16,1024]{3,2,1,0:T(8,128)}, u32[]{:S(2)}, u32[]{:S(2)}) collective-permute-start(f32[2,2,16,1024]{3,2,1,0:T(8,128)} %get-tuple-element.17), channel_id=1, source_target_pairs={{0,1},{1,2},{2,3},{3,4},{4,5},{5,6},{6,7},{7,0},{8,9},{9,10},{10,1... | collective-permute-start | bytes 786440 | tf_op jit(solution)/shard_map/ppermute | solution.py:16
  7.0 30.3 %collective-permute-start.1 = (f32[2,2,16,1024]{3,2,1,0:T(8,128)}, f32[2,2,16,1024]{3,2,1,0:T(8,128)}, u32[]{:S(2)}, u32[]{:S(2)}) collective-permute-start(f32[2,2,16,1024]{3,2,1,0:T(8,128)} %get-tuple-element.18), channel_id=1, source_target_pairs={{1,0},{2,1},{3,2},{4,3},{5,4},{6,5},{7,6},{0,7},{9,8},{10,9},{11,1... | collective-permute-start | bytes 786440 | tf_op jit(solution)/shard_map/ppermute | solution.py:19
  10.5 95.3 %copy-start.59 = (pred[1024]{0:T(1024)(128)(4,1)}, pred[1024]{0:T(1024)(128)(4,1)S(1)}, u32[]{:S(2)}) copy-start(pred[1024]{0:T(1024)(128)(4,1)S(1)} %fusion.647) | copy-start | bytes 3076
  28.5 112.0 %collective-permute-start.4 = (f32[2,8,1,8,512]{4,3,2,1,0:T(8,128)}, f32[2,8,1,8,512]{4,3,2,1,0:T(8,128)}, u32[]{:S(2)}, u32[]{:S(2)}) collective-permute-start(f32[2,8,1,8,512]{4,3,2,1,0:T(8,128)} %get-tuple-element.19), channel_id=1, source_target_pairs={{1,0},{2,1},{3,2},{4,3},{5,4},{6,5},{7,6},{0,7},{9,8},{10,9},{11,1... | collective-permute-start | bytes 786440 | tf_op jit(solution)/shard_map/ppermute | solution.py:19
  30.1 25.5 %collective-permute-start.6 = (f32[2,8,1,16,1024]{4,3,2,1,0:T(8,128)}, f32[2,8,1,16,1024]{4,3,2,1,0:T(8,128)}, u32[]{:S(2)}, u32[]{:S(2)}) collective-permute-start(f32[2,8,1,16,1024]{4,3,2,1,0:T(8,128)} %get-tuple-element.13), channel_id=1, source_target_pairs={{1,0},{2,1},{3,2},{4,3},{5,4},{6,5},{7,6},{0,7},{9,8},{10,9},{11,1... | collective-permute-start | bytes 3145736 | tf_op jit(solution)/shard_map/ppermute | solution.py:19
  31.9 25.5 %collective-permute-start.7 = (f32[2,8,1,16,1024]{4,3,2,1,0:T(8,128)}, f32[2,8,1,16,1024]{4,3,2,1,0:T(8,128)}, u32[]{:S(2)}, u32[]{:S(2)}) collective-permute-start(f32[2,8,1,16,1024]{4,3,2,1,0:T(8,128)} %get-tuple-element.14), channel_id=1, source_target_pairs={{0,1},{1,2},{2,3},{3,4},{4,5},{5,6},{6,7},{7,0},{8,9},{9,10},{10,1... | collective-permute-start | bytes 3145736 | tf_op jit(solution)/shard_map/ppermute | solution.py:16
  36.1 32.5 %copy-start.16 = (f32[1,8,2,8,512]{4,3,2,1,0:T(8,128)}, f32[1,8,2,8,512]{4,3,2,1,0:T(8,128)S(1)}, u32[]{:S(2)}) copy-start(f32[1,8,2,8,512]{4,3,2,1,0:T(8,128)S(1)} %fusion.125) | copy-start | bytes 786436
  36.8 90.5 %copy-start.8 = (f32[4,16,1024]{2,1,0:T(8,128)}, f32[4,16,1024]{2,1,0:T(8,128)S(1)}, u32[]{:S(2)}) copy-start(f32[4,16,1024]{2,1,0:T(8,128)S(1)} %get-tuple-element.38) | copy-start | bytes 786436
  36.9 103.9 %collective-permute-start.5 = (f32[2,8,1,8,512]{4,3,2,1,0:T(8,128)}, f32[2,8,1,8,512]{4,3,2,1,0:T(8,128)}, u32[]{:S(2)}, u32[]{:S(2)}) collective-permute-start(f32[2,8,1,8,512]{4,3,2,1,0:T(8,128)} %get-tuple-element.20), channel_id=1, source_target_pairs={{0,1},{1,2},{2,3},{3,4},{4,5},{5,6},{6,7},{7,0},{8,9},{9,10},{10,1... | collective-permute-start | bytes 786440 | tf_op jit(solution)/shard_map/ppermute | solution.py:16
  38.3 89.0 %copy-start.9 = (f32[4,16,1024]{2,1,0:T(8,128)}, f32[4,16,1024]{2,1,0:T(8,128)S(1)}, u32[]{:S(2)}) copy-start(f32[4,16,1024]{2,1,0:T(8,128)S(1)} %get-tuple-element.15) | copy-start | bytes 786436
  38.3 89.0 %copy-start.10 = (f32[4,16,1024]{2,1,0:T(8,128)}, f32[4,16,1024]{2,1,0:T(8,128)S(1)}, u32[]{:S(2)}) copy-start(f32[4,16,1024]{2,1,0:T(8,128)S(1)} %get-tuple-element.16) | copy-start | bytes 786436
  66.7 23.7 %collective-permute-start.8 = (f32[2,8,1,16,1024]{4,3,2,1,0:T(8,128)}, f32[2,8,1,16,1024]{4,3,2,1,0:T(8,128)}, u32[]{:S(2)}, u32[]{:S(2)}) collective-permute-start(f32[2,8,1,16,1024]{4,3,2,1,0:T(8,128)} %get-tuple-element.11), channel_id=1, source_target_pairs={{1,0},{2,1},{3,2},{4,3},{5,4},{6,5},{7,6},{0,7},{9,8},{10,9},{11,1... | collective-permute-start | bytes 3145736 | tf_op jit(solution)/shard_map/ppermute | solution.py:19
  68.6 25.7 %collective-permute-start.9 = (f32[2,8,1,16,1024]{4,3,2,1,0:T(8,128)}, f32[2,8,1,16,1024]{4,3,2,1,0:T(8,128)}, u32[]{:S(2)}, u32[]{:S(2)}) collective-permute-start(f32[2,8,1,16,1024]{4,3,2,1,0:T(8,128)} %get-tuple-element.12), channel_id=1, source_target_pairs={{0,1},{1,2},{2,3},{3,4},{4,5},{5,6},{6,7},{7,0},{8,9},{9,10},{10,1... | collective-permute-start | bytes 3145736 | tf_op jit(solution)/shard_map/ppermute | solution.py:16
  69.4 73.0 %collective-permute-start.2 = (f32[1,8,1,8,512]{4,3,2,1,0:T(8,128)}, f32[1,8,1,8,512]{4,3,2,1,0:T(8,128)}, u32[]{:S(2)}, u32[]{:S(2)}) collective-permute-start(f32[1,8,1,8,512]{4,3,2,1,0:T(8,128)} %get-tuple-element.41), channel_id=1, source_target_pairs={{1,0},{2,1},{3,2},{4,3},{5,4},{6,5},{7,6},{0,7},{9,8},{10,9},{11,1... | collective-permute-start | bytes 393224 | tf_op jit(solution)/shard_map/ppermute | solution.py:19
  103.6 23.7 %collective-permute-start.10 = (f32[2,8,1,16,1024]{4,3,2,1,0:T(8,128)}, f32[2,8,1,16,1024]{4,3,2,1,0:T(8,128)}, u32[]{:S(2)}, u32[]{:S(2)}) collective-permute-start(f32[2,8,1,16,1024]{4,3,2,1,0:T(8,128)} %get-tuple-element.9), channel_id=1, source_target_pairs={{1,0},{2,1},{3,2},{4,3},{5,4},{6,5},{7,6},{0,7},{9,8},{10,9},{11,1... | collective-permute-start | bytes 3145736 | tf_op jit(solution)/shard_map/ppermute | solution.py:19
  103.6 23.7 %collective-permute-start.11 = (f32[2,8,1,16,1024]{4,3,2,1,0:T(8,128)}, f32[2,8,1,16,1024]{4,3,2,1,0:T(8,128)}, u32[]{:S(2)}, u32[]{:S(2)}) collective-permute-start(f32[2,8,1,16,1024]{4,3,2,1,0:T(8,128)} %get-tuple-element.10), channel_id=1, source_target_pairs={{0,1},{1,2},{2,3},{3,4},{4,5},{5,6},{6,7},{7,0},{8,9},{9,10},{10,1... | collective-permute-start | bytes 3145736 | tf_op jit(solution)/shard_map/ppermute | solution.py:16
  105.8 21.4 %copy-start.7 = (f32[2,8,4,16,1024]{4,3,2,1,0:T(8,128)S(1)}, f32[2,8,4,16,1024]{4,3,2,1,0:T(8,128)}, u32[]{:S(2)}) copy-start(f32[2,8,4,16,1024]{4,3,2,1,0:T(8,128)} %copy-done.6) | copy-start | bytes 12582916
  136.6 21.5 %copy-start.17 = (f32[1,8,2,8,512]{4,3,2,1,0:T(8,128)S(1)}, f32[1,8,2,8,512]{4,3,2,1,0:T(8,128)}, u32[]{:S(2)}) copy-start(f32[1,8,2,8,512]{4,3,2,1,0:T(8,128)} %copy-done.16) | copy-start | bytes 786436
  136.6 21.5 %copy-start.60 = (pred[1024]{0:T(1024)(128)(4,1)S(1)}, pred[1024]{0:T(1024)(128)(4,1)}, u32[]{:S(2)}) copy-start(pred[1024]{0:T(1024)(128)(4,1)} %copy-done.59) | copy-start | bytes 3076
  136.6 21.5 %copy-start.71 = (f32[2,8,512]{2,1,0:T(8,128)S(1)}, f32[2,8,512]{2,1,0:T(8,128)}, u32[]{:S(2)}) copy-start(f32[2,8,512]{2,1,0:T(8,128)} %get-tuple-element.54) | copy-start | bytes 98308
  136.6 31.5 %collective-permute-start.12 = (f32[2,8,1,16,1024]{4,3,2,1,0:T(8,128)}, f32[2,8,1,16,1024]{4,3,2,1,0:T(8,128)}, u32[]{:S(2)}, u32[]{:S(2)}) collective-permute-start(f32[2,8,1,16,1024]{4,3,2,1,0:T(8,128)} %get-tuple-element.7), channel_id=1, source_target_pairs={{1,0},{2,1},{3,2},{4,3},{5,4},{6,5},{7,6},{0,7},{9,8},{10,9},{11,1... | collective-permute-start | bytes 3145736 | tf_op jit(solution)/shard_map/ppermute | solution.py:19
  140.3 27.8 %collective-permute-start.13 = (f32[2,8,1,16,1024]{4,3,2,1,0:T(8,128)}, f32[2,8,1,16,1024]{4,3,2,1,0:T(8,128)}, u32[]{:S(2)}, u32[]{:S(2)}) collective-permute-start(f32[2,8,1,16,1024]{4,3,2,1,0:T(8,128)} %get-tuple-element.8), channel_id=1, source_target_pairs={{0,1},{1,2},{2,3},{3,4},{4,5},{5,6},{6,7},{7,0},{8,9},{9,10},{10,1... | collective-permute-start | bytes 3145736 | tf_op jit(solution)/shard_map/ppermute | solution.py:16
  140.3 21.5 %copy-start.38 = (f32[2,8,512]{2,1,0:T(8,128)}, f32[2,8,512]{2,1,0:T(8,128)S(1)}, u32[]{:S(2)}) copy-start(f32[2,8,512]{2,1,0:T(8,128)S(1)} %get-tuple-element.43) | copy-start | bytes 98308
  140.3 21.5 %copy-start.46 = (f32[2,8,512]{2,1,0:T(8,128)}, f32[2,8,512]{2,1,0:T(8,128)S(1)}, u32[]{:S(2)}) copy-start(f32[2,8,512]{2,1,0:T(8,128)S(1)} %get-tuple-element.44) | copy-start | bytes 98308
  140.4 21.4 %copy-start.20 = (f32[2,8,512]{2,1,0:T(8,128)}, f32[2,8,512]{2,1,0:T(8,128)S(1)}, u32[]{:S(2)}) copy-start(f32[2,8,512]{2,1,0:T(8,128)S(1)} %get-tuple-element.47) | copy-start | bytes 98308
  140.4 21.4 %copy-start.22 = (f32[2,8,512]{2,1,0:T(8,128)}, f32[2,8,512]{2,1,0:T(8,128)S(1)}, u32[]{:S(2)}) copy-start(f32[2,8,512]{2,1,0:T(8,128)S(1)} %get-tuple-element.48) | copy-start | bytes 98308
  140.5 17.6 %collective-permute-start.3 = (f32[1,8,1,8,512]{4,3,2,1,0:T(8,128)S(1)}, f32[1,8,1,8,512]{4,3,2,1,0:T(8,128)S(1)}, u32[]{:S(2)}, u32[]{:S(2)}) collective-permute-start(f32[1,8,1,8,512]{4,3,2,1,0:T(8,128)S(1)} %copy-done.54), channel_id=1, source_target_pairs={{0,1},{1,2},{2,3},{3,4},{4,5},{5,6},{6,7},{7,0},{8,9},{9,10},{10,1... | collective-permute-start | bytes 393224 | tf_op jit(solution)/shard_map/ppermute | solution.py:16
  187.7 5.9 %collective-permute-start.14 = (f32[1,8,1,8,512]{4,3,2,1,0:T(8,128)S(1)}, f32[1,8,1,8,512]{4,3,2,1,0:T(8,128)S(1)}, u32[]{:S(2)}, u32[]{:S(2)}) collective-permute-start(f32[1,8,1,8,512]{4,3,2,1,0:T(8,128)S(1)} %get-tuple-element.33), channel_id=1, source_target_pairs={{1,0},{2,1},{3,2},{4,3},{5,4},{6,5},{7,6},{0,7},{9,8},{10,9},{11,1... | collective-permute-start | bytes 393224 | tf_op jit(solution)/shard_map/ppermute | solution.py:19
  187.8 6.7 %collective-permute-start.15 = (f32[1,8,1,8,512]{4,3,2,1,0:T(8,128)S(1)}, f32[1,8,1,8,512]{4,3,2,1,0:T(8,128)S(1)}, u32[]{:S(2)}, u32[]{:S(2)}) collective-permute-start(f32[1,8,1,8,512]{4,3,2,1,0:T(8,128)S(1)} %get-tuple-element.34), channel_id=1, source_target_pairs={{0,1},{1,2},{2,3},{3,4},{4,5},{5,6},{6,7},{7,0},{8,9},{9,10},{10,1... | collective-permute-start | bytes 393224 | tf_op jit(solution)/shard_map/ppermute | solution.py:16
  204.4 49.7 %copy-start.62 = (pred[1024]{0:T(1024)(128)(4,1)S(1)}, pred[1024]{0:T(1024)(128)(4,1)}, u32[]{:S(2)}) copy-start(pred[1024]{0:T(1024)(128)(4,1)} %copy-done.59) | copy-start | bytes 3076
  204.4 49.7 %copy-start.69 = (f32[8,2,8,512]{3,2,1,0:T(8,128)S(1)}, f32[8,2,8,512]{3,2,1,0:T(8,128)}, u32[]{:S(2)}) copy-start(f32[8,2,8,512]{3,2,1,0:T(8,128)} %copy-done.68) | copy-start | bytes 786436
  204.4 48.9 %collective-permute-start.16 = (f32[8,4,16,1024]{3,2,1,0:T(8,128)S(1)}, f32[8,4,16,1024]{3,2,1,0:T(8,128)S(1)}, u32[]{:S(2)}, u32[]{:S(2)}) collective-permute-start(f32[8,4,16,1024]{3,2,1,0:T(8,128)S(1)} %bitcast_add_fusion.2), channel_id=1, source_target_pairs={{0,8},{8,16},{16,24},{1,9},{9,17},{17,25},{2,10},{10,18},{18,26},{... | collective-permute-start | bytes 6291464 | tf_op jit(solution)/shard_map/ppermute | solution.py:27
  255.7 3.3 collective-permute-start.17
  255.8 6.5 %collective-permute-start.18 = (f32[1,8,1,8,512]{4,3,2,1,0:T(8,128)S(1)}, f32[1,8,1,8,512]{4,3,2,1,0:T(8,128)S(1)}, u32[]{:S(2)}, u32[]{:S(2)}) collective-permute-start(f32[1,8,1,8,512]{4,3,2,1,0:T(8,128)S(1)} %get-tuple-element.32), channel_id=1, source_target_pairs={{0,1},{1,2},{2,3},{3,4},{4,5},{5,6},{6,7},{7,0},{8,9},{9,10},{10,1... | collective-permute-start | bytes 393224 | tf_op jit(solution)/shard_map/ppermute | solution.py:16
  274.5 2.6 collective-permute-start.19
  274.6 6.4 %collective-permute-start.20 = (f32[1,8,1,8,512]{4,3,2,1,0:T(8,128)S(1)}, f32[1,8,1,8,512]{4,3,2,1,0:T(8,128)S(1)}, u32[]{:S(2)}, u32[]{:S(2)}) collective-permute-start(f32[1,8,1,8,512]{4,3,2,1,0:T(8,128)S(1)} %get-tuple-element.30), channel_id=1, source_target_pairs={{0,1},{1,2},{2,3},{3,4},{4,5},{5,6},{6,7},{7,0},{8,9},{9,10},{10,1... | collective-permute-start | bytes 393224 | tf_op jit(solution)/shard_map/ppermute | solution.py:16
  290.8 52.2 %copy-start.64 = (pred[1024]{0:T(1024)(128)(4,1)S(1)}, pred[1024]{0:T(1024)(128)(4,1)}, u32[]{:S(2)}) copy-start(pred[1024]{0:T(1024)(128)(4,1)} %copy-done.59) | copy-start | bytes 3076
  290.8 52.2 %copy-start.70 = (f32[8,2,8,512]{3,2,1,0:T(8,128)S(1)}, f32[8,2,8,512]{3,2,1,0:T(8,128)}, u32[]{:S(2)}) copy-start(f32[8,2,8,512]{3,2,1,0:T(8,128)} %copy-done.68) | copy-start | bytes 786436
  290.8 51.4 %collective-permute-start.21 = (f32[8,4,16,1024]{3,2,1,0:T(8,128)S(1)}, f32[8,4,16,1024]{3,2,1,0:T(8,128)S(1)}, u32[]{:S(2)}, u32[]{:S(2)}) collective-permute-start(f32[8,4,16,1024]{3,2,1,0:T(8,128)S(1)} %bitcast_add_fusion.1), channel_id=1, source_target_pairs={{0,8},{8,16},{16,24},{1,9},{9,17},{17,25},{2,10},{10,18},{18,26},{... | collective-permute-start | bytes 6291464 | tf_op jit(solution)/shard_map/ppermute | solution.py:27
  344.6 2.8 collective-permute-start.22
  344.7 6.2 %collective-permute-start.23 = (f32[1,8,1,8,512]{4,3,2,1,0:T(8,128)S(1)}, f32[1,8,1,8,512]{4,3,2,1,0:T(8,128)S(1)}, u32[]{:S(2)}, u32[]{:S(2)}) collective-permute-start(f32[1,8,1,8,512]{4,3,2,1,0:T(8,128)S(1)} %get-tuple-element.28), channel_id=1, source_target_pairs={{0,1},{1,2},{2,3},{3,4},{4,5},{5,6},{6,7},{7,0},{8,9},{9,10},{10,1... | collective-permute-start | bytes 393224 | tf_op jit(solution)/shard_map/ppermute | solution.py:16
  363.2 3.8 collective-permute-start.24
  363.5 6.2 %collective-permute-start.25 = (f32[1,8,1,8,512]{4,3,2,1,0:T(8,128)S(1)}, f32[1,8,1,8,512]{4,3,2,1,0:T(8,128)S(1)}, u32[]{:S(2)}, u32[]{:S(2)}) collective-permute-start(f32[1,8,1,8,512]{4,3,2,1,0:T(8,128)S(1)} %get-tuple-element.26), channel_id=1, source_target_pairs={{0,1},{1,2},{2,3},{3,4},{4,5},{5,6},{6,7},{7,0},{8,9},{9,10},{10,1... | collective-permute-start | bytes 393224 | tf_op jit(solution)/shard_map/ppermute | solution.py:16
  380.8 47.5 %collective-permute-start.26 = (f32[8,4,16,1024]{3,2,1,0:T(8,128)}, f32[8,4,16,1024]{3,2,1,0:T(8,128)S(1)}, u32[]{:S(2)}, u32[]{:S(2)}) collective-permute-start(f32[8,4,16,1024]{3,2,1,0:T(8,128)} %bitcast_add_fusion), channel_id=1, source_target_pairs={{0,8},{8,16},{16,24},{1,9},{9,17},{17,25},{2,10},{10,18},{18,26},{... | collective-permute-start | bytes 6291464 | tf_op jit(solution)/shard_map/ppermute | solution.py:27
  431.5 4.1 collective-permute-start.27
  433.1 6.2 %collective-permute-start.28 = (f32[1,8,1,8,512]{4,3,2,1,0:T(8,128)S(1)}, f32[1,8,1,8,512]{4,3,2,1,0:T(8,128)S(1)}, u32[]{:S(2)}, u32[]{:S(2)}) collective-permute-start(f32[1,8,1,8,512]{4,3,2,1,0:T(8,128)S(1)} %get-tuple-element.24), channel_id=1, source_target_pairs={{0,1},{1,2},{2,3},{3,4},{4,5},{5,6},{6,7},{7,0},{8,9},{9,10},{10,1... | collective-permute-start | bytes 393224 | tf_op jit(solution)/shard_map/ppermute | solution.py:16
  453.0 3.9 collective-permute-start.29
  453.1 6.5 %collective-permute-start.30 = (f32[1,8,1,8,512]{4,3,2,1,0:T(8,128)S(1)}, f32[1,8,1,8,512]{4,3,2,1,0:T(8,128)S(1)}, u32[]{:S(2)}, u32[]{:S(2)}) collective-permute-start(f32[1,8,1,8,512]{4,3,2,1,0:T(8,128)S(1)} %get-tuple-element.22), channel_id=1, source_target_pairs={{0,1},{1,2},{2,3},{3,4},{4,5},{5,6},{6,7},{7,0},{8,9},{9,10},{10,1... | collective-permute-start | bytes 393224 | tf_op jit(solution)/shard_map/ppermute | solution.py:16
  (55 other events, 460.9 us)
where the time goes:
time: 481 us; the launch traced here: 473 us
  waiting for transfers between devices  243 us (51%)
  other arithmetic  73.6 us (15%)
  local copies, waits for them, and re-layouts  69.8 us (15%)
  matrix products  46.9 us (10%)
  starting transfers between devices  37.9 us (8%)
    ppermute x3, waiting for transfers between devices, shifted_2(): lax.ppermute(value, axis, [(source, source + steps) for source in range(f...  139 us
    ppermute x14, waiting for transfers between devices, extended(): lax.ppermute(lax.slice_in_dim(block, 0, width, axis=dim), axis, backward)  61.6 us
    ppermute x14, waiting for transfers between devices, extended(): lax.ppermute(lax.slice_in_dim(block, block.shape[dim] - width, None, axis...  42 us
    add x5, other arithmetic, explicit_step(): conc + diffusion  36.6 us
    dot_general x12, matrix products, restrict(): jnp.einsum('...z,zw->...w', summed, table, precision=lax.Precision.HIGHEST)  23.5 us
    reshape x9, local copies, waits for them, and re-layouts, prolong(): return grown.reshape(lead + (2 * shape[-3], 2 * shape[-2], shape[-1]))  23.4 us
    dot_general x8, matrix products, prolong(): jnp.einsum('...w,zw->...z', array, table, precision=lax.Precision.HIGHEST)  23.4 us
    ppermute x14, starting transfers between devices, extended(): lax.ppermute(lax.slice_in_dim(block, 0, width, axis=dim), axis, backward)  17 us
  transfers between devices with their start and end apart: 31, of which 23 were waited for; matrix products, arithmetic and copies ran while one was open for 15% of the time, Pallas kernels for 0%

commit v1 on v0

v1 whole, which is shorter than its diff:
```python
import functools

import jax
import jax.numpy as jnp
from jax import lax
from jax.experimental import pallas as pl
from jax.experimental.pallas import tpu as pltpu
from jax.sharding import PartitionSpec as P

PHASES = 4
SUBSTEPS = 4
HIGHEST = lax.Precision.HIGHEST
VMEM = pl.BlockSpec(memory_space=pltpu.VMEM)
SMEM = pl.BlockSpec(memory_space=pltpu.SMEM)


def call(kernel, outs, specs, args, flops):
    shapes = [jax.ShapeDtypeStruct(shape, jnp.float32) for shape in outs]
    moved = sum(a.size * 4 for a in args) + sum(s.size * 4 for s in shapes)
    return pl.pallas_call(
        kernel,
        out_shape=shapes,
        in_specs=specs,
        out_specs=[VMEM] * len(outs),
        compiler_params=pltpu.CompilerParams(vmem_limit_bytes=48 << 20),
        cost_estimate=pl.CostEstimate(flops=flops, bytes_accessed=moved, transcendentals=0),
    )(*args)


def plane_sum(c):
    rows, lanes = c.shape
    row = lax.broadcasted_iota(jnp.int32, c.shape, 0)
    lane = lax.broadcasted_iota(jnp.int32, c.shape, 1)
    zero = jnp.float32(0.0)
    total = jnp.where(row > 0, pltpu.roll(c, 1, 0), zero)
    total = total + jnp.where(row < rows - 1, pltpu.roll(c, rows - 1, 0), zero)
    total = total + jnp.where(lane > 0, pltpu.roll(c, 1, 1), zero)
    return total + jnp.where(lane < lanes - 1, pltpu.roll(c, lanes - 1, 1), zero)


def kappa_of(label, rate_ref):
    kappa = jnp.zeros(label.shape, jnp.float32)
    for phase in range(PHASES):
        kappa = jnp.where(label == phase, rate_ref[phase], kappa)
    return kappa


def fold(a, rows_out):
    rows, lanes = a.shape
    i = lax.broadcasted_iota(jnp.int32, (rows_out, rows), 0)
    j = lax.broadcasted_iota(jnp.int32, (rows_out, rows), 1)
    left = jnp.where(j // 2 == i, jnp.float32(0.125), jnp.float32(0.0))
    y = jnp.dot(left, a, precision=HIGHEST, preferred_element_type=jnp.float32)
    i = lax.broadcasted_iota(jnp.int32, (256, 128), 0)
    j = lax.broadcasted_iota(jnp.int32, (256, 128), 1)
    right = jnp.where(i // 2 == j, jnp.float32(1.0), jnp.float32(0.0))
    return [
        jnp.dot(y[:, g * 256 : g * 256 + 256], right, precision=HIGHEST, preferred_element_type=jnp.float32)
        for g in range(lanes // 256)
    ]


def spread(a):
    rows, lanes = a.shape
    i = lax.broadcasted_iota(jnp.int32, (2 * rows, rows), 0)
    j = lax.broadcasted_iota(jnp.int32, (2 * rows, rows), 1)
    left = jnp.where(i // 2 == j, jnp.float32(1.0), jnp.float32(0.0))
    y = jnp.dot(left, a, precision=HIGHEST, preferred_element_type=jnp.float32)
    i = lax.broadcasted_iota(jnp.int32, (128, 256), 0)
    j = lax.broadcasted_iota(jnp.int32, (128, 256), 1)
    right = jnp.where(j // 2 == i, jnp.float32(1.0), jnp.float32(0.0))
    return [
        jnp.dot(y[:, g * 128 : g * 128 + 128], right, precision=HIGHEST, preferred_element_type=jnp.float32)
        for g in range(lanes // 128)
    ]


def edge_kernel(starts_ref, mask_ref, *outs):
    tile = mask_ref.shape[0]
    spec = starts_ref.shape[1]
    for side, layer in ((0, 0), (1, tile - 1)):
        w = mask_ref[layer].astype(jnp.float32)
        outs[4 + side][0] = w
        for which in range(2):
            for k in range(spec):
                outs[2 * which + side][k, 0] = starts_ref[which, k, layer] * w


def coarse_fields_kernel(mask_ref, label_ref, rate_ref, por_ref, src_ref):
    tile, ny, nz = mask_ref.shape
    pores = mask_ref[...].astype(jnp.float32)
    source = pores * kappa_of(label_ref[...], rate_ref)
    for value, out in ((pores, por_ref), (source, src_ref)):
        pair = value.reshape(tile // 2, 2, ny, nz)
        pair = (pair[:, 0] + pair[:, 1]).reshape(tile // 2 * ny, nz)
        for g, part in enumerate(fold(pair, pair.shape[0] // 2)):
            out[:, :, g * 128 : g * 128 + 128] = part.reshape(tile // 2, ny // 2, 128)


def restrict_kernel(which, merge, *refs):
    if merge:
        starts_ref, mask_ref, u_ref, prev_ref, out_ref = refs
    else:
        starts_ref, out_ref = refs
    _, spec, tile, ny, nz = starts_ref.shape

    def layer(k, i):
        if merge:
            return jnp.where(mask_ref[i] != 0, u_ref[k, i], starts_ref[which, k, i])
        return starts_ref[which, k, i]

    for k in range(spec):
        pair = jnp.concatenate(
            [layer(k, 2 * i) + layer(k, 2 * i + 1) for i in range(tile // 2)], axis=0
        )
        for g, part in enumerate(fold(pair, pair.shape[0] // 2)):
            part = part.reshape(tile // 2, ny // 2, 128)
            lanes = slice(g * 128, g * 128 + 128)
            if merge:
                part = part - prev_ref[k, :, :, lanes]
            out_ref[k, :, :, lanes] = part


def fine_kernel(
    first, u_ref, lo_ref, hi_ref, mask_ref, wlo_ref, whi_ref, label_ref,
    rate_ref, d_ref, st_ref, out_ref, elo_ref, ehi_ref, w_s, wide_s, src_s,
):
    tile = mask_ref.shape[0]
    spec = out_ref.shape[0]

    def cell(k, i):
        if i < 0:
            return lo_ref[k, 0]
        if i >= tile:
            return hi_ref[k, 0]
        if first is not None:
            return u_ref[first, k, i] * w_s[i]
        return u_ref[k, i]

    for i in range(tile):
        w_s[i] = mask_ref[i].astype(jnp.float32)
    for i in range(tile):
        below = w_s[i - 1] if i else wlo_ref[0]
        above = w_s[i + 1] if i + 1 < tile else whi_ref[0]
        wide_s[i] = w_s[i] * (plane_sum(w_s[i]) + below + above)
        source = w_s[i] * kappa_of(label_ref[i], rate_ref)
        src_s[i] = source * (1.0 - cell(0, i) * cell(1, i))

    def body(k, carry):
        d = d_ref[k]
        st = st_ref[k]
        for i in range(tile):
            c = cell(k, i)
            total = plane_sum(c) + cell(k, i - 1) + cell(k, i + 1)
            new = c + d * (w_s[i] * total - wide_s[i] * c) + st * src_s[i]
            out_ref[k, i] = new
            if i == 0:
                elo_ref[k, 0] = new
            if i == tile - 1:
                ehi_ref[k, 0] = new
        return carry

    lax.fori_loop(0, spec, body, 0)


def coarse_step(cell, por, src, d_ref, st_ref, spec, layers, emit):
    for i in layers:
        p = por(i)
        wide = p * (plane_sum(p) + por(i - 1) + por(i + 1))
        below, above = por(i - 1), por(i + 1)
        rate = float(SUBSTEPS) * (src(i) * (1.0 - cell(0, i) * cell(1, i)))
        for k in range(spec):
            c = cell(k, i)
            total = plane_sum(p * c) + below * cell(k, i - 1) + above * cell(k, i + 1)
            emit(k, i, c + d_ref[k] * (p * total - wide * c) + st_ref[k] * rate)


def section_kernel(
    lo, own, hi, q1lo, q1, q1hi, q2, prev1, prev2, plo, p, phi, slo, s, shi,
    d_ref, st_ref, next_ref, d1_ref, d2_ref, mid,
):
    spec = own.shape[0]

    def tri(a, b, c, n):
        return lambda i: a[i + n] if i < 0 else (b[i] if i < 2 else c[i - 2])

    def tri_k(a, b, c, n):
        return lambda k, i: a[k, i + n] if i < 0 else (b[k, i] if i < 2 else c[k, i - 2])

    por = tri(plo, p, phi, 2)
    src = tri(slo, s, shi, 1)
    q = tri_k(q1lo, q1, q1hi, 1)

    def first(k, i, g):
        mid[k, i + 1] = g + q(k, i)
        if 0 <= i < 2:
            d1_ref[k, i] = g - prev1[k, i]

    coarse_step(tri_k(lo, own, hi, 2), por, src, d_ref, st_ref, spec, (-1, 0, 1, 2), first)

    def second(k, i, g):
        next_ref[k, i] = g + q2[k, i]
        d2_ref[k, i] = g - prev2[k, i]

    coarse_step(lambda k, i: mid[k, i + 1], por, src, d_ref, st_ref, spec, (0, 1), second)


def prev_kernel(lo, own, hi, plo, p, phi, s, d_ref, st_ref, out_ref):
    spec = own.shape[0]
    last = lo.shape[1]

    def cell(k, i):
        return lo[k, last - 1] if i < 0 else (own[k, i] if i < 2 else hi[k, 0])

    def por(i):
        return plo[1] if i < 0 else (p[i] if i < 2 else phi[0])

    def emit(k, i, g):
        out_ref[k, i] = g

    coarse_step(cell, por, lambda i: s[i], d_ref, st_ref, spec, (0, 1), emit)


def final_kernel(starts_ref, mask_ref, ua_ref, ub_ref, da_ref, db_ref, out_ref):
    _, tile, ny, nz = starts_ref.shape
    _, half, cy, cz = da_ref.shape
    which = pl.program_id(0)

    def write(u_ref, delta_ref):
        for g, part in enumerate(spread(delta_ref[0].reshape(half * cy, cz))):
            part = part.reshape(half, ny, 256)
            lanes = slice(g * 256, g * 256 + 256)
            for i in range(tile):
                fine = jnp.where(mask_ref[i, :, lanes] != 0, u_ref[0, i, :, lanes], starts_ref[0, i, :, lanes])
                out_ref[0, i, :, lanes] = part[i // 2] + fine

    @pl.when(which == 0)
    def _():
        write(ua_ref, da_ref)

    @pl.when(which == 1)
    def _():
        write(ub_ref, db_ref)


def final(starts, mask, ua, ub, da, db):
    count, spec, tile, ny, nz = starts.shape
    a = lambda n, k: (jnp.where(n == 0, k, spec - 1), 0, 0, 0)
    b = lambda n, k: (jnp.where(n == 0, 0, k), 0, 0, 0)
    fine = (1, tile, ny, nz)
    coarse = (1,) + da.shape[1:]
    return pl.pallas_call(
        final_kernel,
        grid=(count, spec),
        out_shape=jax.ShapeDtypeStruct(starts.shape, jnp.float32),
        in_specs=[
            pl.BlockSpec((None,) + fine, lambda n, k: (n, k, 0, 0, 0)),
            pl.BlockSpec((tile, ny, nz), lambda n, k: (0, 0, 0)),
            pl.BlockSpec(fine, a),
            pl.BlockSpec(fine, b),
            pl.BlockSpec(coarse, a),
            pl.BlockSpec(coarse, b),
        ],
        out_specs=pl.BlockSpec((None,) + fine, lambda n, k: (n, k, 0, 0, 0)),
        cost_estimate=pl.CostEstimate(flops=4 * starts.size, bytes_accessed=12 * starts.size, transcendentals=0),
    )(starts, mask, ua, ub, da, db)


def around(low_part, high_part):
    count = lax.axis_size("space")
    up = [(i, (i + 1) % count) for i in range(count)]
    down = [(target, source) for source, target in up]
    return lax.ppermute(high_part, "space", up), lax.ppermute(low_part, "space", down)


def local(starts, mask, label, diffusivity, stoich, rate):
    _, spec, tile, ny, nz = starts.shape
    edge = (spec, 1, ny, nz)
    state = (spec, tile, ny, nz)
    coarse = (spec, tile // 2, ny // 2, nz // 2)
    plane = (tile // 2, ny // 2, nz // 2)

    ea_lo, ea_hi, eb_lo, eb_hi, w_lo, w_hi = call(
        edge_kernel, [edge] * 4 + [(1, ny, nz)] * 2, [VMEM] * 2, (starts, mask), 1 << 20
    )
    wb, wa = around(w_lo, w_hi)
    halo = [around(ea_lo, ea_hi), around(eb_lo, eb_hi)]
    por, src = call(
        coarse_fields_kernel, [plane] * 2, [VMEM, VMEM, SMEM], (mask, label, rate), 1 << 26
    )
    pb, pa = around(por, por)
    sb, sa = around(src[:1], src[1:])
    rs = [
        call(functools.partial(restrict_kernel, n, False), [coarse], [VMEM], (starts,), 1 << 28)[0]
        for n in range(2)
    ]
    v_lo, v_hi = around(rs[0], rs[0])
    r_lo, r_hi = around(rs[1][:, :1], rs[1][:, 1:])

    def previous(lo, own, hi):
        return call(
            prev_kernel, [coarse], [VMEM] * 7 + [SMEM] * 2,
            (lo, own, hi, pb, por, pa, src, diffusivity, stoich), 1 << 22,
        )[0]

    states = [starts, starts]
    prev = [None, None]
    for turn in range(SUBSTEPS):
        for n in range(2):
            below, above = halo[n]
            args = (states[n], below, above, mask, wb, wa, label, rate, diffusivity, stoich)
            first = n if turn == 0 else None
            shapes = [jax.ShapeDtypeStruct(x, jnp.float32) for x in (state, edge, edge)]
            states[n], e_lo, e_hi = pl.pallas_call(
                functools.partial(fine_kernel, first),
                out_shape=shapes,
                in_specs=[VMEM] * 7 + [SMEM] * 3,
                out_specs=[VMEM] * 3,
                scratch_shapes=[pltpu.VMEM((tile, ny, nz), jnp.float32)] * 3,
                compiler_params=pltpu.CompilerParams(vmem_limit_bytes=32 << 20),
                cost_estimate=pl.CostEstimate(flops=1 << 24, bytes_accessed=6 << 20, transcendentals=0),
            )(*args)
            if turn + 1 < SUBSTEPS:
                halo[n] = around(e_lo, e_hi)
    prev[0] = previous(v_lo, rs[0], v_hi)
    prev[1] = previous(r_lo, rs[1], r_hi)
    q = [
        call(
            functools.partial(restrict_kernel, n, True), [coarse], [VMEM] * 4,
            (starts, mask, states[n], prev[n]), 1 << 28,
        )[0]
        for n in range(2)
    ]
    q_lo, q_hi = around(q[0][:, :1], q[0][:, 1:])

    def section(lo, own, hi):
        return pl.pallas_call(
            section_kernel,
            out_shape=[jax.ShapeDtypeStruct(coarse, jnp.float32)] * 3,
            in_specs=[VMEM] * 15 + [SMEM] * 2,
            out_specs=[VMEM] * 3,
            scratch_shapes=[pltpu.VMEM((spec, tile // 2 + 2) + coarse[2:], jnp.float32)],
            cost_estimate=pl.CostEstimate(flops=1 << 22, bytes_accessed=2 << 20, transcendentals=0),
        )(lo, own, hi, q_lo, q[0], q_hi, q[1], prev[0], prev[1], pb, por, pa, sb, src, sa, diffusivity, stoich)

    place = lax.axis_index("tm")
    sections = lax.axis_size("tm")
    count = lax.axis_size("space")
    current = [jnp.where(place == 0, x, 0.0) for x in (v_lo, rs[0], v_hi)]
    for target in range(1, sections):
        out = section(*current)[0]
        base, there = (target - 1) * count, target * count
        for slot, step in ((0, 1), (1, 0), (2, -1)):
            pairs = [(base + i, there + (i + step) % count) for i in range(count)]
            current[slot] = current[slot] + lax.ppermute(out, ("tm", "space"), pairs)
    _, delta_a, delta_b = section(*current)
    return final(starts, mask, states[0], states[1], delta_a, delta_b)


def solution(mesh):
    placed = (
        P("tm", None, "space", None, None),
        P("space", None, None),
        P("space", None, None),
        P(),
        P(),
        P(),
    )
    return jax.shard_map(
        local,
        mesh=mesh,
        in_specs=placed,
        out_specs=P("tm", None, "space", None, None),
        check_vma=False,
    )
```

time: 481 us -> 226 us (0.47); the launches traced: 473 us -> 224 us
  waiting for transfers between devices: 243 us -> 77.6 us
  Pallas kernels: 0 us -> 77.8 us
  other arithmetic: 73.6 us -> 8.95 us
  local copies, waits for them, and re-layouts: 69.8 us -> 12.1 us
  matrix products: 46.9 us -> 0 us
  starting transfers between devices: 37.9 us -> 46.8 us
    ppermute x31 -> x37, waiting for transfers between devices: 243 us -> 77.6 us  [the longest x9 42 us: local(): current[slot] = current[slot] + lax.ppermute(out, ('tm', 'space'), pairs)]
    pallas_call x0 -> x21, Pallas kernels: none -> 77.8 us  [the longest x8 26.5 us: local(): pl.pallas_call(functools.partial(fine_kernel, first), out_shape=shapes, i...]
    add x25 -> x9, other arithmetic: 61.6 us -> 6.76 us  [local(): current[slot] = current[slot] + lax.ppermute(out, ('tm', 'space'), pairs)]
    dot_general x20 -> x0, matrix products: 46.9 us -> none  [the longest x12 23.5 us: restrict(): jnp.einsum('...z,zw->...w', summed, table, precision=lax.Precision.HIGHEST)]
    slice x39 -> x3, local copies, waits for them, and re-layouts: 25.6 us -> 0.75 us  [the longest x1 0.72 us: local(): r_lo, r_hi = around(rs[1][:, :1], rs[1][:, 1:])]
    reshape x9 -> x0, local copies, waits for them, and re-layouts: 23.4 us -> none  [prolong(): return grown.reshape(lead + (2 * shape[-3], 2 * shape[-2], shape[-1]))]
    broadcast_in_dim x8 -> x0, local copies, waits for them, and re-layouts: 15.5 us -> none  [prolong(): jnp.broadcast_to(spread[..., :, None, :, None, :], lead + (shape[-3], 2,...]
    mul x15 -> x0, other arithmetic: 9.19 us -> none  [the longest x6 4.57 us: explicit_step(): rscale * stoich[:, None, None, None] * rate[..., None, :, :, :]]
  transfers between devices with their start and end apart: 31 -> 37, of which waited for: 23 -> 10; matrix products, arithmetic and copies ran while one was open for 15% -> 3% of each run, Pallas kernels for 0% -> 21%
where the time goes in v1:
time: 226 us; the launch traced here: 224 us
  Pallas kernels  77.8 us (34%)
  waiting for transfers between devices  77.6 us (34%)
  starting transfers between devices  46.8 us (21%)
  local copies, waits for them, and re-layouts  12.1 us (5%)
  other arithmetic  8.95 us (4%)
    ppermute x9, waiting for transfers between devices, local(): current[slot] = current[slot] + lax.ppermute(out, ('tm', 'space'), pairs)  42 us
    ppermute x14, starting transfers between devices, around(): lax.ppermute(low_part, 'space', down)  30.5 us
    pallas_call x8, Pallas kernels, local(): pl.pallas_call(functools.partial(fine_kernel, first), out_shape=shapes, i...  26.5 us
    ppermute x14, waiting for transfers between devices, around(): lax.ppermute(high_part, 'space', up)  26.3 us
    pallas_call x8, Pallas kernels, call(): pl.pallas_call(kernel, out_shape=shapes, in_specs=specs, out_specs=[VMEM]...  23.7 us
    pallas_call x1, Pallas kernels, final(): pl.pallas_call(final_kernel, grid=(count, spec), out_shape=jax.ShapeDtype...  15 us
    pallas_call x4, Pallas kernels, section(): pl.pallas_call(section_kernel, out_shape=[jax.ShapeDtypeStruct(coarse, jn...  12.5 us
    unnamed x92, local copies, waits for them, and re-layouts  11.3 us
  transfers between devices with their start and end apart: 37, of which 10 were waited for; matrix products, arithmetic and copies ran while one was open for 3% of the time, Pallas kernels for 21%

profile of v1, /device:TPU:4, one launch (start us, length us, event | category | flops | bytes accessed | tf_op | source)
XLA Modules:
  0.0 223.9 jit_solution(1624631802700813366)
XLA Ops:
  1.1 2.6 %shard_map.64 = (f32[8,1,16,1024]{3,2,1,0:T(8,128)S(1)}, f32[8,1,16,1024]{3,2,1,0:T(8,128)S(1)}, f32[8,1,16,1024]{3,2,1,0:T(8,128)S(1)}, f32[8,1,16,1024]{3,2,1,...) custom-call(f32[2,8,4,16,1024]{4,3,2,1,0:T(8,128)} %starts_ref.3, s32[4,16,1024]{2,1,0:T(8,128)S(1)} %copy-done.2), custom_call_target="tpu_custom_call" | custom-call | flops 1048576 | bytes 6684672 | tf_op jit(solution)/shard_map/pallas_call | solution.py:20
  3.8 3.5 %collective-permute-start.1 = (f32[8,1,16,1024]{3,2,1,0:T(8,128)S(1)}, f32[8,1,16,1024]{3,2,1,0:T(8,128)S(1)}, u32[]{:S(2)}, u32[]{:S(2)}) collective-permute-start(f32[8,1,16,1024]{3,2,1,0:T(8,128)S(1)} %get-tuple-element.39), channel_id=1, source_target_pairs={{1,0},{2,1},{3,2},{4,3},{5,4},{6,5},{7,6},{0,7},{9,8},{10,9},{11,1... | collective-permute-start | bytes 1572872 | tf_op jit(solution)/shard_map/ppermute | solution.py:273
  7.3 3.5 %collective-permute-start.11 = (f32[8,1,16,1024]{3,2,1,0:T(8,128)S(1)}, f32[8,1,16,1024]{3,2,1,0:T(8,128)S(1)}, u32[]{:S(2)}, u32[]{:S(2)}) collective-permute-start(f32[8,1,16,1024]{3,2,1,0:T(8,128)S(1)} %get-tuple-element.53), channel_id=1, source_target_pairs={{1,0},{2,1},{3,2},{4,3},{5,4},{6,5},{7,6},{0,7},{9,8},{10,9},{11,1... | collective-permute-start | bytes 1572872 | tf_op jit(solution)/shard_map/ppermute | solution.py:273
  10.8 19.4 %collective-permute-done.2.wlo_ref = f32[1,16,1024]{2,1,0:T(8,128)S(1)} collective-permute-done((f32[1,16,1024]{2,1,0:T(8,128)S(1)}, f32[1,16,1024]{2,1,0:T(8,128)S(1)}, u32[]{:S(2)}, u32[]{:S(2)}) %collective-permute-start.2) | collective-permute-done | bytes 65568 | tf_op jit(solution)/shard_map/ppermute | solution.py:273
  30.3 1.9 collective-permute-done.3.whi_ref
  32.2 2.9 %shard_map.65 = (f32[8,4,16,1024]{3,2,1,0:T(8,128)S(1)}, f32[8,1,16,1024]{3,2,1,0:T(8,128)S(1)}, f32[8,1,16,1024]{3,2,1,0:T(8,128)S(1)}) custom-call(f32[2,8,4,16,1024]{4,3,2,1,0:T(8,128)S(1)} %copy-done, f32[8,1,16,1024]{3,2,1,0:T(8,128)S(1)} %collective-permute-done.lo_ref, f32[8,1,16,1024]{3,2,1,0:T(8,128)S(1)} %collective-permute-done.1.hi_ref, ...), custom_call_target="tpu_custom_call" | custom-call | flops 16777216 | bytes 6291456 | tf_op jit(solution)/shard_map/pallas_call | solution.py:314
  35.3 3.6 %collective-permute-start.5 = (f32[8,1,16,1024]{3,2,1,0:T(8,128)S(1)}, f32[8,1,16,1024]{3,2,1,0:T(8,128)S(1)}, u32[]{:S(2)}, u32[]{:S(2)}) collective-permute-start(f32[8,1,16,1024]{3,2,1,0:T(8,128)S(1)} %get-tuple-element.44), channel_id=1, source_target_pairs={{1,0},{2,1},{3,2},{4,3},{5,4},{6,5},{7,6},{0,7},{9,8},{10,9},{11,1... | collective-permute-start | bytes 1572872 | tf_op jit(solution)/shard_map/ppermute | solution.py:273
  38.9 2.9 %shard_map.69 = (f32[8,4,16,1024]{3,2,1,0:T(8,128)S(1)}, f32[8,1,16,1024]{3,2,1,0:T(8,128)S(1)}, f32[8,1,16,1024]{3,2,1,0:T(8,128)S(1)}) custom-call(f32[2,8,4,16,1024]{4,3,2,1,0:T(8,128)S(1)} %copy-done, f32[8,1,16,1024]{3,2,1,0:T(8,128)S(1)} %collective-permute-done.10.lo_ref, f32[8,1,16,1024]{3,2,1,0:T(8,128)S(1)} %collective-permute-done.11.hi_ref, ...), custom_call_target="tpu_custom_call" | custom-call | flops 16777216 | bytes 6291456 | tf_op jit(solution)/shard_map/pallas_call | solution.py:314
  41.8 3.5 %collective-permute-start.13 = (f32[8,1,16,1024]{3,2,1,0:T(8,128)S(1)}, f32[8,1,16,1024]{3,2,1,0:T(8,128)S(1)}, u32[]{:S(2)}, u32[]{:S(2)}) collective-permute-start(f32[8,1,16,1024]{3,2,1,0:T(8,128)S(1)} %get-tuple-element.56), channel_id=1, source_target_pairs={{1,0},{2,1},{3,2},{4,3},{5,4},{6,5},{7,6},{0,7},{9,8},{10,9},{11,1... | collective-permute-start | bytes 1572872 | tf_op jit(solution)/shard_map/ppermute | solution.py:273
  45.3 4.0 %collective-permute-done.4.lo_ref = f32[8,1,16,1024]{3,2,1,0:T(8,128)S(1)} collective-permute-done((f32[8,1,16,1024]{3,2,1,0:T(8,128)S(1)}, f32[8,1,16,1024]{3,2,1,0:T(8,128)S(1)}, u32[]{:S(2)}, u32[]{:S(2)}) %collective-permute-start.4) | collective-permute-done | bytes 524320 | tf_op jit(solution)/shard_map/ppermute | solution.py:273
  49.4 1.9 collective-permute-done.5.hi_ref
  51.2 3.0 %shard_map.66 = (f32[8,4,16,1024]{3,2,1,0:T(8,128)S(1)}, f32[8,1,16,1024]{3,2,1,0:T(8,128)S(1)}, f32[8,1,16,1024]{3,2,1,0:T(8,128)S(1)}) custom-call(f32[8,4,16,1024]{3,2,1,0:T(8,128)S(1)} %get-tuple-element.42.u_ref, f32[8,1,16,1024]{3,2,1,0:T(8,128)S(1)} %collective-permute-done.4.lo_ref, f32[8,1,16,1024]{3,2,1,0:T(8,128)S(1)} %collective-permute-done.5.hi_ref, ...), custom_call_target="tpu_custom_call" | custom-call | flops 16777216 | bytes 6291456 | tf_op jit(solution)/shard_map/pallas_call | solution.py:314
  54.2 1.5 collective-permute-start.6
  55.7 2.4 %collective-permute-start.7 = (f32[8,1,16,1024]{3,2,1,0:T(8,128)S(1)}, f32[8,1,16,1024]{3,2,1,0:T(8,128)S(1)}, u32[]{:S(2)}, u32[]{:S(2)}) collective-permute-start(f32[8,1,16,1024]{3,2,1,0:T(8,128)S(1)} %get-tuple-element.47), channel_id=1, source_target_pairs={{1,0},{2,1},{3,2},{4,3},{5,4},{6,5},{7,6},{0,7},{9,8},{10,9},{11,1... | collective-permute-start | bytes 1572872 | tf_op jit(solution)/shard_map/ppermute | solution.py:273
  58.0 1.4 shard_map.74
  59.5 3.0 %shard_map.77.own = f32[8,2,8,512]{3,2,1,0:T(8,128)S(1)} custom-call(f32[2,8,4,16,1024]{4,3,2,1,0:T(8,128)S(1)} %copy-done), custom_call_target="tpu_custom_call" | custom-call | flops 268435456 | bytes 4456448 | tf_op jit(solution)/shard_map/pallas_call | solution.py:20
  62.5 3.8 %shard_map.70 = (f32[8,4,16,1024]{3,2,1,0:T(8,128)S(1)}, f32[8,1,16,1024]{3,2,1,0:T(8,128)}, f32[8,1,16,1024]{3,2,1,0:T(8,128)}) custom-call(f32[8,4,16,1024]{3,2,1,0:T(8,128)S(1)} %get-tuple-element.54.u_ref, f32[8,1,16,1024]{3,2,1,0:T(8,128)S(1)} %collective-permute-done.12.lo_ref, f32[8,1,16,1024]{3,2,1,0:T(8,128)S(1)} %collective-permute-done.13.hi_ref, ...), custom_call_target="tpu_custom_call" | custom-call | flops 16777216 | bytes 6291456 | tf_op jit(solution)/shard_map/pallas_call | solution.py:314
  66.3 1.3 copy-done.17
  67.6 1.4 collective-permute-start.14
  69.7 2.8 %collective-permute-done.20.plo = f32[2,8,512]{2,1,0:T(8,128)S(1)} collective-permute-done((f32[2,8,512]{2,1,0:T(8,128)S(1)}, f32[2,8,512]{2,1,0:T(8,128)S(1)}, u32[]{:S(2)}, u32[]{:S(2)}) %collective-permute-start.20) | collective-permute-done | bytes 32800 | tf_op jit(solution)/shard_map/ppermute | solution.py:273
  74.0 2.4 %collective-permute-start.15 = (f32[8,1,16,1024]{3,2,1,0:T(8,128)}, f32[8,1,16,1024]{3,2,1,0:T(8,128)}, u32[]{:S(2)}, u32[]{:S(2)}) collective-permute-start(f32[8,1,16,1024]{3,2,1,0:T(8,128)} %get-tuple-element.59), channel_id=1, source_target_pairs={{1,0},{2,1},{3,2},{4,3},{5,4},{6,5},{7,6},{0,7},{9,8},{10,9},{11,1... | collective-permute-start | bytes 1572872 | tf_op jit(solution)/shard_map/ppermute | solution.py:273
  77.3 2.2 copy-done.1
  79.5 2.9 %shard_map.73.own = f32[8,2,8,512]{3,2,1,0:T(8,128)S(1)} custom-call(f32[2,8,4,16,1024]{4,3,2,1,0:T(8,128)S(1)} %copy-done.1), custom_call_target="tpu_custom_call" | custom-call | flops 268435456 | bytes 4456448 | tf_op jit(solution)/shard_map/pallas_call | solution.py:20
  82.5 2.7 %shard_map.67 = (f32[8,4,16,1024]{3,2,1,0:T(8,128)S(1)}, f32[8,1,16,1024]{3,2,1,0:T(8,128)S(1)}, f32[8,1,16,1024]{3,2,1,0:T(8,128)S(1)}) custom-call(f32[8,4,16,1024]{3,2,1,0:T(8,128)S(1)} %get-tuple-element.45.u_ref, f32[8,1,16,1024]{3,2,1,0:T(8,128)S(1)} %copy-done.28, f32[8,1,16,1024]{3,2,1,0:T(8,128)S(1)} %copy-done.30, s32[4,16,1024]{2,1,0:T(8,128)S(1)} %copy-done.3, ...), custom_call_target="tpu_custom_call" | custom-call | flops 16777216 | bytes 6291456 | tf_op jit(solution)/shard_map/pallas_call | solution.py:314
  85.3 2.7 %collective-permute-start.18 = (f32[8,2,8,512]{3,2,1,0:T(8,128)S(1)}, f32[8,2,8,512]{3,2,1,0:T(8,128)S(1)}, u32[]{:S(2)}, u32[]{:S(2)}) collective-permute-start(f32[8,2,8,512]{3,2,1,0:T(8,128)S(1)} %shard_map.73.own), channel_id=1, source_target_pairs={{0,1},{1,2},{2,3},{3,4},{4,5},{5,6},{6,7},{7,0},{8,9},{9,10},{10,1... | collective-permute-start | bytes 786440 | tf_op jit(solution)/shard_map/ppermute | solution.py:273
  88.1 3.5 %collective-permute-start.9 = (f32[8,1,16,1024]{3,2,1,0:T(8,128)S(1)}, f32[8,1,16,1024]{3,2,1,0:T(8,128)S(1)}, u32[]{:S(2)}, u32[]{:S(2)}) collective-permute-start(f32[8,1,16,1024]{3,2,1,0:T(8,128)S(1)} %get-tuple-element.50), channel_id=1, source_target_pairs={{1,0},{2,1},{3,2},{4,3},{5,4},{6,5},{7,6},{0,7},{9,8},{10,9},{11,1... | collective-permute-start | bytes 1572872 | tf_op jit(solution)/shard_map/ppermute | solution.py:273
  96.0 3.7 %shard_map.71 = (f32[8,4,16,1024]{3,2,1,0:T(8,128)S(1)}, f32[8,1,16,1024]{3,2,1,0:T(8,128)S(1)}, f32[8,1,16,1024]{3,2,1,0:T(8,128)S(1)}) custom-call(f32[8,4,16,1024]{3,2,1,0:T(8,128)S(1)} %copy-done.18, f32[8,1,16,1024]{3,2,1,0:T(8,128)} %collective-permute-done.14.lo_ref, f32[8,1,16,1024]{3,2,1,0:T(8,128)} %collective-permute-done.15.hi_ref, ...), custom_call_target="tpu_custom_call" | custom-call | flops 16777216 | bytes 6291456 | tf_op jit(solution)/shard_map/pallas_call | solution.py:314
  100.2 3.1 %collective-permute-start.17 = (f32[8,1,16,1024]{3,2,1,0:T(8,128)S(1)}, f32[8,1,16,1024]{3,2,1,0:T(8,128)S(1)}, u32[]{:S(2)}, u32[]{:S(2)}) collective-permute-start(f32[8,1,16,1024]{3,2,1,0:T(8,128)S(1)} %get-tuple-element.62), channel_id=1, source_target_pairs={{1,0},{2,1},{3,2},{4,3},{5,4},{6,5},{7,6},{0,7},{9,8},{10,9},{11,1... | collective-permute-start | bytes 1572872 | tf_op jit(solution)/shard_map/ppermute | solution.py:273
  104.0 5.5 %collective-permute-done.19.hi = f32[8,2,8,512]{3,2,1,0:T(8,128)S(1)} collective-permute-done((f32[8,2,8,512]{3,2,1,0:T(8,128)S(1)}, f32[8,2,8,512]{3,2,1,0:T(8,128)S(1)}, u32[]{:S(2)}, u32[]{:S(2)}) %collective-permute-start.19) | collective-permute-done | bytes 262176 | tf_op jit(solution)/shard_map/ppermute | solution.py:273
  110.4 3.8 %shard_map.68 = (f32[8,4,16,1024]{3,2,1,0:T(8,128)S(1)}, f32[8,1,16,1024]{3,2,1,0:T(8,128)}, f32[8,1,16,1024]{3,2,1,0:T(8,128)}) custom-call(f32[8,4,16,1024]{3,2,1,0:T(8,128)S(1)} %get-tuple-element.48.u_ref, f32[8,1,16,1024]{3,2,1,0:T(8,128)S(1)} %collective-permute-done.8.lo_ref, f32[8,1,16,1024]{3,2,1,0:T(8,128)S(1)} %collective-permute-done.9.hi_ref, ...), custom_call_target="tpu_custom_call" | custom-call | flops 16777216 | bytes 6291456 | tf_op jit(solution)/shard_map/pallas_call | solution.py:314
  114.2 5.9 %shard_map.76.q1 = f32[8,2,8,512]{3,2,1,0:T(8,128)S(1)} custom-call(f32[2,8,4,16,1024]{4,3,2,1,0:T(8,128)} %starts_ref.3, s32[4,16,1024]{2,1,0:T(8,128)S(1)} %copy-done.3, f32[8,4,16,1024]{3,2,1,0:T(8,128)S(1)} %get-tuple-element.51.refs_2_.ua_ref, f32[8,2,8,512]{3,2,1,0:T(8,128)S(1)} %shard_map.75.refs_3_.prev1), custom_call_target="tpu_custom_call" | custom-call | flops 268435456 | bytes 7077888 | tf_op jit(solution)/shard_map/pallas_call | solution.py:20
  120.3 3.8 %collective-permute-start.23 = (f32[8,1,8,512]{3,2,1,0:T(8,128)S(1)}, f32[8,1,8,512]{3,2,1,0:T(8,128)S(1)}, u32[]{:S(2)}, u32[]{:S(2)}) collective-permute-start(f32[8,1,8,512]{3,2,1,0:T(8,128)S(1)} %get-tuple-element.73), channel_id=1, source_target_pairs={{1,0},{2,1},{3,2},{4,3},{5,4},{6,5},{7,6},{0,7},{9,8},{10,9},{11,1... | collective-permute-start | bytes 393224 | tf_op jit(solution)/shard_map/ppermute | solution.py:273
  125.3 3.8 %shard_map.72 = (f32[8,4,16,1024]{3,2,1,0:T(8,128)S(1)}, f32[8,1,16,1024]{3,2,1,0:T(8,128)}, f32[8,1,16,1024]{3,2,1,0:T(8,128)}) custom-call(f32[8,4,16,1024]{3,2,1,0:T(8,128)S(1)} %get-tuple-element.60.u_ref, f32[8,1,16,1024]{3,2,1,0:T(8,128)S(1)} %collective-permute-done.16.lo_ref, f32[8,1,16,1024]{3,2,1,0:T(8,128)S(1)} %collective-permute-done.17.hi_ref, ...), custom_call_target="tpu_custom_call" | custom-call | flops 16777216 | bytes 6291456 | tf_op jit(solution)/shard_map/pallas_call | solution.py:314
  129.1 5.9 %shard_map.79.q2 = f32[8,2,8,512]{3,2,1,0:T(8,128)S(1)} custom-call(f32[2,8,4,16,1024]{4,3,2,1,0:T(8,128)} %starts_ref.3, s32[4,16,1024]{2,1,0:T(8,128)S(1)} %copy-done.3, f32[8,4,16,1024]{3,2,1,0:T(8,128)S(1)} %get-tuple-element.63.refs_2_.ub_ref, f32[8,2,8,512]{3,2,1,0:T(8,128)S(1)} %shard_map.78.refs_3_.prev2), custom_call_target="tpu_custom_call" | custom-call | flops 268435456 | bytes 7077888 | tf_op jit(solution)/shard_map/pallas_call | solution.py:20
  137.7 3.1 %shard_map.80 = (f32[8,2,8,512]{3,2,1,0:T(8,128)}, f32[8,2,8,512]{3,2,1,0:T(8,128)}, f32[8,2,8,512]{3,2,1,0:T(8,128)}) custom-call(f32[8,2,8,512]{3,2,1,0:T(8,128)} %broadcast_select_fusion.2.lo, f32[8,2,8,512]{3,2,1,0:T(8,128)} %broadcast_select_fusion.1.own, f32[8,2,8,512]{3,2,1,0:T(8,128)} %broadcast_select_fusion.hi, f32[8,1,8,512]{3,2,1,0:T(8,128)} %copy-done.42, ...), custom_call_target="tpu_custom_call" | custom-call | flops 4194304 | bytes 2097152 | tf_op jit(solution)/shard_map/pallas_call | solution.py:337
  145.1 3.1 %shard_map.81 = (f32[8,2,8,512]{3,2,1,0:T(8,128)}, f32[8,2,8,512]{3,2,1,0:T(8,128)}, f32[8,2,8,512]{3,2,1,0:T(8,128)}) custom-call(f32[8,2,8,512]{3,2,1,0:T(8,128)} %fusion.5.lo, f32[8,2,8,512]{3,2,1,0:T(8,128)} %fusion.4.own, f32[8,2,8,512]{3,2,1,0:T(8,128)} %fusion.3.hi, f32[8,1,8,512]{3,2,1,0:T(8,128)} %copy-done.42, f32[8,2,8,512]{3,2,1,0:T(8,128)} %copy-done.5, ...), custom_call_target="tpu_custom_call" | custom-call | flops 4194304 | bytes 2097152 | tf_op jit(solution)/shard_map/pallas_call | solution.py:337
  149.6 1.3 collective-permute-start.32
  150.9 1.3 collective-permute-start.33
  152.2 18.4 %collective-permute-done.31 = f32[8,2,8,512]{3,2,1,0:T(8,128)S(1)} collective-permute-done((f32[8,2,8,512]{3,2,1,0:T(8,128)}, f32[8,2,8,512]{3,2,1,0:T(8,128)S(1)}, u32[]{:S(2)}, u32[]{:S(2)}) %collective-permute-start.31) | collective-permute-done | bytes 262176 | tf_op jit(solution)/shard_map/ppermute | solution.py:355
  171.3 13.2 %collective-permute-done.32 = f32[8,2,8,512]{3,2,1,0:T(8,128)S(1)} collective-permute-done((f32[8,2,8,512]{3,2,1,0:T(8,128)}, f32[8,2,8,512]{3,2,1,0:T(8,128)S(1)}, u32[]{:S(2)}, u32[]{:S(2)}) %collective-permute-start.32) | collective-permute-done | bytes 262176 | tf_op jit(solution)/shard_map/ppermute | solution.py:355
  186.0 3.1 %shard_map.82 = (f32[8,2,8,512]{3,2,1,0:T(8,128)}, f32[8,2,8,512]{3,2,1,0:T(8,128)}, f32[8,2,8,512]{3,2,1,0:T(8,128)}) custom-call(f32[8,2,8,512]{3,2,1,0:T(8,128)} %add.30.lo, f32[8,2,8,512]{3,2,1,0:T(8,128)} %add.31.own, f32[8,2,8,512]{3,2,1,0:T(8,128)} %add.32.hi, f32[8,1,8,512]{3,2,1,0:T(8,128)} %copy-done.42, f32[8,2,8,512]{3,2,1,0:T(8,128)} %copy-done.5, ...), custom_call_target="tpu_custom_call" | custom-call | flops 4194304 | bytes 2097152 | tf_op jit(solution)/shard_map/pallas_call | solution.py:337
  189.2 1.3 collective-permute-start.34
  190.5 1.3 collective-permute-start.35
  191.8 1.3 collective-permute-start.36
  193.1 7.2 %collective-permute-done.34 = f32[8,2,8,512]{3,2,1,0:T(8,128)S(1)} collective-permute-done((f32[8,2,8,512]{3,2,1,0:T(8,128)}, f32[8,2,8,512]{3,2,1,0:T(8,128)S(1)}, u32[]{:S(2)}, u32[]{:S(2)}) %collective-permute-start.34) | collective-permute-done | bytes 262176 | tf_op jit(solution)/shard_map/ppermute | solution.py:355
  201.1 3.2 %collective-permute-done.35 = f32[8,2,8,512]{3,2,1,0:T(8,128)S(1)} collective-permute-done((f32[8,2,8,512]{3,2,1,0:T(8,128)}, f32[8,2,8,512]{3,2,1,0:T(8,128)S(1)}, u32[]{:S(2)}, u32[]{:S(2)}) %collective-permute-start.35) | collective-permute-done | bytes 262176 | tf_op jit(solution)/shard_map/ppermute | solution.py:355
  205.8 3.1 %shard_map.83 = (f32[8,2,8,512]{3,2,1,0:T(8,128)}, f32[8,2,8,512]{3,2,1,0:T(8,128)}, f32[8,2,8,512]{3,2,1,0:T(8,128)}) custom-call(f32[8,2,8,512]{3,2,1,0:T(8,128)} %add.33.lo, f32[8,2,8,512]{3,2,1,0:T(8,128)} %add.34.own, f32[8,2,8,512]{3,2,1,0:T(8,128)} %add.35.hi, f32[8,1,8,512]{3,2,1,0:T(8,128)} %copy-done.42, f32[8,2,8,512]{3,2,1,0:T(8,128)} %copy-done.5, ...), custom_call_target="tpu_custom_call" | custom-call | flops 4194304 | bytes 2097152 | tf_op jit(solution)/shard_map/pallas_call | solution.py:337
  208.9 15.0 %shard_map.84 = f32[2,8,4,16,1024]{4,3,2,1,0:T(8,128)} custom-call(f32[2,8,4,16,1024]{4,3,2,1,0:T(8,128)} %starts_ref.3, s32[4,16,1024]{2,1,0:T(8,128)} %mask_ref.21, f32[8,4,16,1024]{3,2,1,0:T(8,128)} %copy-done.8, f32[8,4,16,1024]{3,2,1,0:T(8,128)} %copy-done.9, f32[8,2,8,512]{3,2,1,0:T(8,128)} %get-tuple-element.69.da_ref, ...), custom_call_target="tpu_custom_call" | custom-call | flops 4194304 | bytes 12582912 | tf_op jit(solution)/shard_map/pallas_call | solution.py:252
  (154 shorter events, 25.0 us)
Async XLA Ops:
  0.0 32.2 %copy-start = (f32[2,8,4,16,1024]{4,3,2,1,0:T(8,128)S(1)}, f32[2,8,4,16,1024]{4,3,2,1,0:T(8,128)}, u32[]{:S(2)}) copy-start(f32[2,8,4,16,1024]{4,3,2,1,0:T(8,128)} %starts_ref.3) | copy-start | bytes 12582916
  1.1 31.1 %copy-start.4 = (s32[4,16,1024]{2,1,0:T(8,128)S(1)}, s32[4,16,1024]{2,1,0:T(8,128)}, u32[]{:S(2)}) copy-start(s32[4,16,1024]{2,1,0:T(8,128)} %label_ref.17) | copy-start | bytes 786436
  1.1 31.1 %copy-start.33 = (f32[8]{0:T(128)S(1)}, f32[8]{0:T(128)}, u32[]{:S(2)}) copy-start(f32[8]{0:T(128)} %d_ref.27) | copy-start | bytes 100
  1.1 31.1 %copy-start.34 = (f32[8]{0:T(128)S(1)}, f32[8]{0:T(128)}, u32[]{:S(2)}) copy-start(f32[8]{0:T(128)} %st_ref.27) | copy-start | bytes 100
  1.1 31.1 %copy-start.35 = (f32[4]{0:T(128)S(1)}, f32[4]{0:T(128)}, u32[]{:S(2)}) copy-start(f32[4]{0:T(128)} %rate_ref.17) | copy-start | bytes 52
  3.7 28.5 %collective-permute-start = (f32[8,1,16,1024]{3,2,1,0:T(8,128)S(1)}, f32[8,1,16,1024]{3,2,1,0:T(8,128)S(1)}, u32[]{:S(2)}, u32[]{:S(2)}) collective-permute-start(f32[8,1,16,1024]{3,2,1,0:T(8,128)S(1)} %get-tuple-element.38), channel_id=1, source_target_pairs={{0,1},{1,2},{2,3},{3,4},{4,5},{5,6},{6,7},{7,0},{8,9},{9,10},{10,1... | collective-permute-start | bytes 1572872 | tf_op jit(solution)/shard_map/ppermute | solution.py:273
  3.8 28.4 %collective-permute-start.1 = (f32[8,1,16,1024]{3,2,1,0:T(8,128)S(1)}, f32[8,1,16,1024]{3,2,1,0:T(8,128)S(1)}, u32[]{:S(2)}, u32[]{:S(2)}) collective-permute-start(f32[8,1,16,1024]{3,2,1,0:T(8,128)S(1)} %get-tuple-element.39), channel_id=1, source_target_pairs={{1,0},{2,1},{3,2},{4,3},{5,4},{6,5},{7,6},{0,7},{9,8},{10,9},{11,1... | collective-permute-start | bytes 1572872 | tf_op jit(solution)/shard_map/ppermute | solution.py:273
  7.3 31.6 %collective-permute-start.10 = (f32[8,1,16,1024]{3,2,1,0:T(8,128)S(1)}, f32[8,1,16,1024]{3,2,1,0:T(8,128)S(1)}, u32[]{:S(2)}, u32[]{:S(2)}) collective-permute-start(f32[8,1,16,1024]{3,2,1,0:T(8,128)S(1)} %get-tuple-element.52), channel_id=1, source_target_pairs={{0,1},{1,2},{2,3},{3,4},{4,5},{5,6},{6,7},{7,0},{8,9},{9,10},{10,1... | collective-permute-start | bytes 1572872 | tf_op jit(solution)/shard_map/ppermute | solution.py:273
  7.3 31.6 %collective-permute-start.11 = (f32[8,1,16,1024]{3,2,1,0:T(8,128)S(1)}, f32[8,1,16,1024]{3,2,1,0:T(8,128)S(1)}, u32[]{:S(2)}, u32[]{:S(2)}) collective-permute-start(f32[8,1,16,1024]{3,2,1,0:T(8,128)S(1)} %get-tuple-element.53), channel_id=1, source_target_pairs={{1,0},{2,1},{3,2},{4,3},{5,4},{6,5},{7,6},{0,7},{9,8},{10,9},{11,1... | collective-permute-start | bytes 1572872 | tf_op jit(solution)/shard_map/ppermute | solution.py:273
  10.8 19.4 %collective-permute-start.2 = (f32[1,16,1024]{2,1,0:T(8,128)S(1)}, f32[1,16,1024]{2,1,0:T(8,128)S(1)}, u32[]{:S(2)}, u32[]{:S(2)}) collective-permute-start(f32[1,16,1024]{2,1,0:T(8,128)S(1)} %get-tuple-element.40), channel_id=1, source_target_pairs={{0,1},{1,2},{2,3},{3,4},{4,5},{5,6},{6,7},{7,0},{8,9},{9,10},{10,1... | collective-permute-start | bytes 196616 | tf_op jit(solution)/shard_map/ppermute | solution.py:273
  30.2 1.9 collective-permute-start.3
  35.1 14.2 %collective-permute-start.4 = (f32[8,1,16,1024]{3,2,1,0:T(8,128)S(1)}, f32[8,1,16,1024]{3,2,1,0:T(8,128)S(1)}, u32[]{:S(2)}, u32[]{:S(2)}) collective-permute-start(f32[8,1,16,1024]{3,2,1,0:T(8,128)S(1)} %get-tuple-element.43), channel_id=1, source_target_pairs={{0,1},{1,2},{2,3},{3,4},{4,5},{5,6},{6,7},{7,0},{8,9},{9,10},{10,1... | collective-permute-start | bytes 1572872 | tf_op jit(solution)/shard_map/ppermute | solution.py:273
  35.3 16.0 %collective-permute-start.5 = (f32[8,1,16,1024]{3,2,1,0:T(8,128)S(1)}, f32[8,1,16,1024]{3,2,1,0:T(8,128)S(1)}, u32[]{:S(2)}, u32[]{:S(2)}) collective-permute-start(f32[8,1,16,1024]{3,2,1,0:T(8,128)S(1)} %get-tuple-element.44), channel_id=1, source_target_pairs={{1,0},{2,1},{3,2},{4,3},{5,4},{6,5},{7,6},{0,7},{9,8},{10,9},{11,1... | collective-permute-start | bytes 1572872 | tf_op jit(solution)/shard_map/ppermute | solution.py:273
  41.7 20.7 %collective-permute-start.12 = (f32[8,1,16,1024]{3,2,1,0:T(8,128)S(1)}, f32[8,1,16,1024]{3,2,1,0:T(8,128)S(1)}, u32[]{:S(2)}, u32[]{:S(2)}) collective-permute-start(f32[8,1,16,1024]{3,2,1,0:T(8,128)S(1)} %get-tuple-element.55), channel_id=1, source_target_pairs={{0,1},{1,2},{2,3},{3,4},{4,5},{5,6},{6,7},{7,0},{8,9},{9,10},{10,1... | collective-permute-start | bytes 1572872 | tf_op jit(solution)/shard_map/ppermute | solution.py:273
  41.8 20.7 %collective-permute-start.13 = (f32[8,1,16,1024]{3,2,1,0:T(8,128)S(1)}, f32[8,1,16,1024]{3,2,1,0:T(8,128)S(1)}, u32[]{:S(2)}, u32[]{:S(2)}) collective-permute-start(f32[8,1,16,1024]{3,2,1,0:T(8,128)S(1)} %get-tuple-element.56), channel_id=1, source_target_pairs={{1,0},{2,1},{3,2},{4,3},{5,4},{6,5},{7,6},{0,7},{9,8},{10,9},{11,1... | collective-permute-start | bytes 1572872 | tf_op jit(solution)/shard_map/ppermute | solution.py:273
  54.2 19.0 %collective-permute-start.6 = (f32[8,1,16,1024]{3,2,1,0:T(8,128)S(1)}, f32[8,1,16,1024]{3,2,1,0:T(8,128)S(1)}, u32[]{:S(2)}, u32[]{:S(2)}) collective-permute-start(f32[8,1,16,1024]{3,2,1,0:T(8,128)S(1)} %get-tuple-element.46), channel_id=1, source_target_pairs={{0,1},{1,2},{2,3},{3,4},{4,5},{5,6},{6,7},{7,0},{8,9},{9,10},{10,1... | collective-permute-start | bytes 1572872 | tf_op jit(solution)/shard_map/ppermute | solution.py:273
  55.7 20.8 %collective-permute-start.7 = (f32[8,1,16,1024]{3,2,1,0:T(8,128)S(1)}, f32[8,1,16,1024]{3,2,1,0:T(8,128)S(1)}, u32[]{:S(2)}, u32[]{:S(2)}) collective-permute-start(f32[8,1,16,1024]{3,2,1,0:T(8,128)S(1)} %get-tuple-element.47), channel_id=1, source_target_pairs={{1,0},{2,1},{3,2},{4,3},{5,4},{6,5},{7,6},{0,7},{9,8},{10,9},{11,1... | collective-permute-start | bytes 1572872 | tf_op jit(solution)/shard_map/ppermute | solution.py:273
  59.4 32.8 %copy-start.19 = (f32[2,8,512]{2,1,0:T(8,128)}, f32[2,8,512]{2,1,0:T(8,128)S(1)}, u32[]{:S(2)}) copy-start(f32[2,8,512]{2,1,0:T(8,128)S(1)} %get-tuple-element.65.s) | copy-start | bytes 98308
  59.5 13.1 %collective-permute-start.20 = (f32[2,8,512]{2,1,0:T(8,128)S(1)}, f32[2,8,512]{2,1,0:T(8,128)S(1)}, u32[]{:S(2)}, u32[]{:S(2)}) collective-permute-start(f32[2,8,512]{2,1,0:T(8,128)S(1)} %get-tuple-element.64.p), channel_id=1, source_target_pairs={{0,1},{1,2},{2,3},{3,4},{4,5},{5,6},{6,7},{7,0},{8,9},{9,10},{10,1... | collective-permute-start | bytes 98312 | tf_op jit(solution)/shard_map/ppermute | solution.py:273
  67.6 24.7 %collective-permute-start.14 = (f32[8,1,16,1024]{3,2,1,0:T(8,128)}, f32[8,1,16,1024]{3,2,1,0:T(8,128)}, u32[]{:S(2)}, u32[]{:S(2)}) collective-permute-start(f32[8,1,16,1024]{3,2,1,0:T(8,128)} %get-tuple-element.58), channel_id=1, source_target_pairs={{0,1},{1,2},{2,3},{3,4},{4,5},{5,6},{6,7},{7,0},{8,9},{9,10},{10,1... | collective-permute-start | bytes 1572872 | tf_op jit(solution)/shard_map/ppermute | solution.py:273
  69.7 18.3 %collective-permute-start.24 = (f32[8,1,8,512]{3,2,1,0:T(8,128)}, f32[8,1,8,512]{3,2,1,0:T(8,128)S(1)}, u32[]{:S(2)}, u32[]{:S(2)}) collective-permute-start(f32[8,1,8,512]{3,2,1,0:T(8,128)} %get-tuple-element.72), channel_id=1, source_target_pairs={{0,1},{1,2},{2,3},{3,4},{4,5},{5,6},{6,7},{7,0},{8,9},{9,10},{10,1... | collective-permute-start | bytes 393224 | tf_op jit(solution)/shard_map/ppermute | solution.py:273
  72.5 15.5 %collective-permute-start.25 = (f32[8,1,8,512]{3,2,1,0:T(8,128)}, f32[8,1,8,512]{3,2,1,0:T(8,128)}, u32[]{:S(2)}, u32[]{:S(2)}) collective-permute-start(f32[8,1,8,512]{3,2,1,0:T(8,128)} %get-tuple-element.71), channel_id=1, source_target_pairs={{1,0},{2,1},{3,2},{4,3},{5,4},{6,5},{7,6},{0,7},{9,8},{10,9},{11,1... | collective-permute-start | bytes 393224 | tf_op jit(solution)/shard_map/ppermute | solution.py:273
  74.0 21.9 %collective-permute-start.15 = (f32[8,1,16,1024]{3,2,1,0:T(8,128)}, f32[8,1,16,1024]{3,2,1,0:T(8,128)}, u32[]{:S(2)}, u32[]{:S(2)}) collective-permute-start(f32[8,1,16,1024]{3,2,1,0:T(8,128)} %get-tuple-element.59), channel_id=1, source_target_pairs={{1,0},{2,1},{3,2},{4,3},{5,4},{6,5},{7,6},{0,7},{9,8},{10,9},{11,1... | collective-permute-start | bytes 1572872 | tf_op jit(solution)/shard_map/ppermute | solution.py:273
  77.3 8.0 %collective-permute-start.21 = (f32[2,8,512]{2,1,0:T(8,128)S(1)}, f32[2,8,512]{2,1,0:T(8,128)S(1)}, u32[]{:S(2)}, u32[]{:S(2)}) collective-permute-start(f32[2,8,512]{2,1,0:T(8,128)S(1)} %get-tuple-element.64.p), channel_id=1, source_target_pairs={{1,0},{2,1},{3,2},{4,3},{5,4},{6,5},{7,6},{0,7},{9,8},{10,9},{11,1... | collective-permute-start | bytes 98312 | tf_op jit(solution)/shard_map/ppermute | solution.py:273
  82.4 27.1 %copy-start.11 = (f32[8,2,8,512]{3,2,1,0:T(8,128)}, f32[8,2,8,512]{3,2,1,0:T(8,128)S(1)}, u32[]{:S(2)}) copy-start(f32[8,2,8,512]{3,2,1,0:T(8,128)S(1)} %shard_map.73.own) | copy-start | bytes 786436
  85.3 14.9 %collective-permute-start.18 = (f32[8,2,8,512]{3,2,1,0:T(8,128)S(1)}, f32[8,2,8,512]{3,2,1,0:T(8,128)S(1)}, u32[]{:S(2)}, u32[]{:S(2)}) collective-permute-start(f32[8,2,8,512]{3,2,1,0:T(8,128)S(1)} %shard_map.73.own), channel_id=1, source_target_pairs={{0,1},{1,2},{2,3},{3,4},{4,5},{5,6},{6,7},{7,0},{8,9},{9,10},{10,1... | collective-permute-start | bytes 786440 | tf_op jit(solution)/shard_map/ppermute | solution.py:273
  88.0 22.4 %collective-permute-start.8 = (f32[8,1,16,1024]{3,2,1,0:T(8,128)S(1)}, f32[8,1,16,1024]{3,2,1,0:T(8,128)S(1)}, u32[]{:S(2)}, u32[]{:S(2)}) collective-permute-start(f32[8,1,16,1024]{3,2,1,0:T(8,128)S(1)} %get-tuple-element.49), channel_id=1, source_target_pairs={{0,1},{1,2},{2,3},{3,4},{4,5},{5,6},{6,7},{7,0},{8,9},{9,10},{10,1... | collective-permute-start | bytes 1572872 | tf_op jit(solution)/shard_map/ppermute | solution.py:273
  88.1 22.3 %collective-permute-start.9 = (f32[8,1,16,1024]{3,2,1,0:T(8,128)S(1)}, f32[8,1,16,1024]{3,2,1,0:T(8,128)S(1)}, u32[]{:S(2)}, u32[]{:S(2)}) collective-permute-start(f32[8,1,16,1024]{3,2,1,0:T(8,128)S(1)} %get-tuple-element.50), channel_id=1, source_target_pairs={{1,0},{2,1},{3,2},{4,3},{5,4},{6,5},{7,6},{0,7},{9,8},{10,9},{11,1... | collective-permute-start | bytes 1572872 | tf_op jit(solution)/shard_map/ppermute | solution.py:273
  92.3 17.3 %collective-permute-start.19 = (f32[8,2,8,512]{3,2,1,0:T(8,128)S(1)}, f32[8,2,8,512]{3,2,1,0:T(8,128)S(1)}, u32[]{:S(2)}, u32[]{:S(2)}) collective-permute-start(f32[8,2,8,512]{3,2,1,0:T(8,128)S(1)} %shard_map.73.own), channel_id=1, source_target_pairs={{1,0},{2,1},{3,2},{4,3},{5,4},{6,5},{7,6},{0,7},{9,8},{10,9},{11,1... | collective-permute-start | bytes 786440 | tf_op jit(solution)/shard_map/ppermute | solution.py:273
  95.9 33.1 %copy-start.6 = (f32[8,2,8,512]{3,2,1,0:T(8,128)}, f32[8,2,8,512]{3,2,1,0:T(8,128)S(1)}, u32[]{:S(2)}) copy-start(f32[8,2,8,512]{3,2,1,0:T(8,128)S(1)} %shard_map.78.refs_3_.prev2) | copy-start | bytes 786436
  99.7 25.1 %collective-permute-start.16 = (f32[8,1,16,1024]{3,2,1,0:T(8,128)S(1)}, f32[8,1,16,1024]{3,2,1,0:T(8,128)S(1)}, u32[]{:S(2)}, u32[]{:S(2)}) collective-permute-start(f32[8,1,16,1024]{3,2,1,0:T(8,128)S(1)} %get-tuple-element.61), channel_id=1, source_target_pairs={{0,1},{1,2},{2,3},{3,4},{4,5},{5,6},{6,7},{7,0},{8,9},{9,10},{10,1... | collective-permute-start | bytes 1572872 | tf_op jit(solution)/shard_map/ppermute | solution.py:273
  100.2 25.0 %collective-permute-start.17 = (f32[8,1,16,1024]{3,2,1,0:T(8,128)S(1)}, f32[8,1,16,1024]{3,2,1,0:T(8,128)S(1)}, u32[]{:S(2)}, u32[]{:S(2)}) collective-permute-start(f32[8,1,16,1024]{3,2,1,0:T(8,128)S(1)} %get-tuple-element.62), channel_id=1, source_target_pairs={{1,0},{2,1},{3,2},{4,3},{5,4},{6,5},{7,6},{0,7},{9,8},{10,9},{11,1... | collective-permute-start | bytes 1572872 | tf_op jit(solution)/shard_map/ppermute | solution.py:273
  109.5 26.2 %collective-permute-start.26 = (f32[1,8,512]{2,1,0:T(8,128)S(1)}, f32[1,8,512]{2,1,0:T(8,128)S(1)}, u32[]{:S(2)}, u32[]{:S(2)}) collective-permute-start(f32[1,8,512]{2,1,0:T(8,128)S(1)} %get-tuple-element.76), channel_id=1, source_target_pairs={{0,1},{1,2},{2,3},{3,4},{4,5},{5,6},{6,7},{7,0},{8,9},{9,10},{10,1... | collective-permute-start | bytes 49160 | tf_op jit(solution)/shard_map/ppermute | solution.py:273
  120.2 15.6 %collective-permute-start.22 = (f32[8,1,8,512]{3,2,1,0:T(8,128)S(1)}, f32[8,1,8,512]{3,2,1,0:T(8,128)S(1)}, u32[]{:S(2)}, u32[]{:S(2)}) collective-permute-start(f32[8,1,8,512]{3,2,1,0:T(8,128)S(1)} %get-tuple-element.74), channel_id=1, source_target_pairs={{0,1},{1,2},{2,3},{3,4},{4,5},{5,6},{6,7},{7,0},{8,9},{9,10},{10,1... | collective-permute-start | bytes 393224 | tf_op jit(solution)/shard_map/ppermute | solution.py:273
  120.3 16.1 %collective-permute-start.23 = (f32[8,1,8,512]{3,2,1,0:T(8,128)S(1)}, f32[8,1,8,512]{3,2,1,0:T(8,128)S(1)}, u32[]{:S(2)}, u32[]{:S(2)}) collective-permute-start(f32[8,1,8,512]{3,2,1,0:T(8,128)S(1)} %get-tuple-element.73), channel_id=1, source_target_pairs={{1,0},{2,1},{3,2},{4,3},{5,4},{6,5},{7,6},{0,7},{9,8},{10,9},{11,1... | collective-permute-start | bytes 393224 | tf_op jit(solution)/shard_map/ppermute | solution.py:273
  124.8 11.0 %collective-permute-start.27 = (f32[1,8,512]{2,1,0:T(8,128)S(1)}, f32[1,8,512]{2,1,0:T(8,128)S(1)}, u32[]{:S(2)}, u32[]{:S(2)}) collective-permute-start(f32[1,8,512]{2,1,0:T(8,128)S(1)} %get-tuple-element.75), channel_id=1, source_target_pairs={{1,0},{2,1},{3,2},{4,3},{5,4},{6,5},{7,6},{0,7},{9,8},{10,9},{11,1... | collective-permute-start | bytes 49160 | tf_op jit(solution)/shard_map/ppermute | solution.py:273
  140.8 2.0 collective-permute-start.28
  141.5 2.2 collective-permute-start.29
  142.1 2.2 collective-permute-start.30
  144.4 40.1 %copy-start.40 = (f32[8,2,8,512]{3,2,1,0:T(8,128)S(1)}, f32[8,2,8,512]{3,2,1,0:T(8,128)}, u32[]{:S(2)}) copy-start(f32[8,2,8,512]{3,2,1,0:T(8,128)} %fusion.4.own) | copy-start | bytes 786436
  145.1 40.1 %copy-start.41 = (f32[8,2,8,512]{3,2,1,0:T(8,128)S(1)}, f32[8,2,8,512]{3,2,1,0:T(8,128)}, u32[]{:S(2)}) copy-start(f32[8,2,8,512]{3,2,1,0:T(8,128)} %fusion.3.hi) | copy-start | bytes 786436
  148.3 22.3 %collective-permute-start.31 = (f32[8,2,8,512]{3,2,1,0:T(8,128)}, f32[8,2,8,512]{3,2,1,0:T(8,128)S(1)}, u32[]{:S(2)}, u32[]{:S(2)}) collective-permute-start(f32[8,2,8,512]{3,2,1,0:T(8,128)} %get-tuple-element.67), channel_id=1, source_target_pairs={{8,17},{9,18},{10,19},{11,20},{12,21},{13,22},{14,23},{15,16}} | collective-permute-start | bytes 786440 | tf_op jit(solution)/shard_map/ppermute | solution.py:355
  149.6 34.9 %collective-permute-start.32 = (f32[8,2,8,512]{3,2,1,0:T(8,128)}, f32[8,2,8,512]{3,2,1,0:T(8,128)S(1)}, u32[]{:S(2)}, u32[]{:S(2)}) collective-permute-start(f32[8,2,8,512]{3,2,1,0:T(8,128)} %get-tuple-element.67), channel_id=1, source_target_pairs={{8,16},{9,17},{10,18},{11,19},{12,20},{13,21},{14,22},{15,23}} | collective-permute-start | bytes 786440 | tf_op jit(solution)/shard_map/ppermute | solution.py:355
  150.9 34.4 %collective-permute-start.33 = (f32[8,2,8,512]{3,2,1,0:T(8,128)}, f32[8,2,8,512]{3,2,1,0:T(8,128)S(1)}, u32[]{:S(2)}, u32[]{:S(2)}) collective-permute-start(f32[8,2,8,512]{3,2,1,0:T(8,128)} %get-tuple-element.67), channel_id=1, source_target_pairs={{8,23},{9,16},{10,17},{11,18},{12,19},{13,20},{14,21},{15,22}} | collective-permute-start | bytes 786440 | tf_op jit(solution)/shard_map/ppermute | solution.py:355
  171.3 29.0 %copy-start.36 = (f32[8,2,8,512]{3,2,1,0:T(8,128)S(1)}, f32[8,2,8,512]{3,2,1,0:T(8,128)}, u32[]{:S(2)}) copy-start(f32[8,2,8,512]{3,2,1,0:T(8,128)} %add.30.lo) | copy-start | bytes 786436
  189.2 11.2 %collective-permute-start.34 = (f32[8,2,8,512]{3,2,1,0:T(8,128)}, f32[8,2,8,512]{3,2,1,0:T(8,128)S(1)}, u32[]{:S(2)}, u32[]{:S(2)}) collective-permute-start(f32[8,2,8,512]{3,2,1,0:T(8,128)} %get-tuple-element.68), channel_id=1, source_target_pairs={{16,25},{17,26},{18,27},{19,28},{20,29},{21,30},{22,31},{23,24}} | collective-permute-start | bytes 786440 | tf_op jit(solution)/shard_map/ppermute | solution.py:355
  190.5 13.8 %collective-permute-start.35 = (f32[8,2,8,512]{3,2,1,0:T(8,128)}, f32[8,2,8,512]{3,2,1,0:T(8,128)S(1)}, u32[]{:S(2)}, u32[]{:S(2)}) collective-permute-start(f32[8,2,8,512]{3,2,1,0:T(8,128)} %get-tuple-element.68), channel_id=1, source_target_pairs={{16,24},{17,25},{18,26},{19,27},{20,28},{21,29},{22,30},{23,31}} | collective-permute-start | bytes 786440 | tf_op jit(solution)/shard_map/ppermute | solution.py:355
  191.8 13.2 %collective-permute-start.36 = (f32[8,2,8,512]{3,2,1,0:T(8,128)}, f32[8,2,8,512]{3,2,1,0:T(8,128)S(1)}, u32[]{:S(2)}, u32[]{:S(2)}) collective-permute-start(f32[8,2,8,512]{3,2,1,0:T(8,128)} %get-tuple-element.68), channel_id=1, source_target_pairs={{16,31},{17,24},{18,25},{19,26},{20,27},{21,28},{22,29},{23,30}} | collective-permute-start | bytes 786440 | tf_op jit(solution)/shard_map/ppermute | solution.py:355
  (35 other events, 236.1 us)

commit v2 on v1

v2 whole, which is shorter than its diff:
```python
import functools

import jax
import jax.numpy as jnp
from jax import lax
from jax.experimental import pallas as pl
from jax.experimental.pallas import tpu as pltpu
from jax.sharding import PartitionSpec as P

PHASES = 4
SUBSTEPS = 4
VMEM = pl.BlockSpec(memory_space=pltpu.VMEM)
SMEM = pl.BlockSpec(memory_space=pltpu.SMEM)


def call(kernel, outs, specs, args, flops):
    shapes = [jax.ShapeDtypeStruct(shape, jnp.float32) for shape in outs]
    moved = sum(a.size * 4 for a in args) + sum(s.size * 4 for s in shapes)
    return pl.pallas_call(
        kernel,
        out_shape=shapes,
        in_specs=specs,
        out_specs=[VMEM] * len(outs),
        compiler_params=pltpu.CompilerParams(vmem_limit_bytes=48 << 20),
        cost_estimate=pl.CostEstimate(flops=flops, bytes_accessed=moved, transcendentals=0),
    )(*args)


def plane_sum(c):
    rows, lanes = c.shape
    row = lax.broadcasted_iota(jnp.int32, c.shape, 0)
    lane = lax.broadcasted_iota(jnp.int32, c.shape, 1)
    zero = jnp.float32(0.0)
    total = jnp.where(row > 0, pltpu.roll(c, 1, 0), zero)
    total = total + jnp.where(row < rows - 1, pltpu.roll(c, rows - 1, 0), zero)
    total = total + jnp.where(lane > 0, pltpu.roll(c, 1, 1), zero)
    return total + jnp.where(lane < lanes - 1, pltpu.roll(c, lanes - 1, 1), zero)


def kappa_of(label, rate_ref):
    kappa = jnp.zeros(label.shape, jnp.float32)
    for phase in range(PHASES):
        kappa = jnp.where(label == phase, rate_ref[phase], kappa)
    return kappa


def pieces(a):
    high = a.astype(jnp.bfloat16)
    rest = a - high.astype(jnp.float32)
    middle = rest.astype(jnp.bfloat16)
    low = (rest - middle.astype(jnp.float32)).astype(jnp.bfloat16)
    return low, middle, high


def table(shape, value):
    i = lax.broadcasted_iota(jnp.int32, shape, 0)
    j = lax.broadcasted_iota(jnp.int32, shape, 1)
    same = (i // 2 == j) if shape[0] > shape[1] else (j // 2 == i)
    return jnp.where(same, jnp.float32(value), jnp.float32(0.0)).astype(jnp.bfloat16)


def times(a, right):
    return sum(jnp.dot(x, right, preferred_element_type=jnp.float32) for x in pieces(a))


def from_left(left, a):
    return sum(jnp.dot(left, x, preferred_element_type=jnp.float32) for x in pieces(a))


def fold(a):
    rows, lanes = a.shape
    left = table((rows // 2, rows), 0.125)
    right = table((256, 128), 1.0)
    return [from_left(left, times(a[:, g * 256 : g * 256 + 256], right)) for g in range(lanes // 256)]


def spread(a):
    rows, lanes = a.shape
    y = from_left(table((2 * rows, rows), 1.0), a)
    right = table((128, 256), 1.0)
    return [times(y[:, g * 128 : g * 128 + 128], right) for g in range(lanes // 128)]


def edge_kernel(starts_ref, mask_ref, *outs):
    tile = mask_ref.shape[0]
    spec = starts_ref.shape[1]
    for side, layer in ((0, 0), (1, tile - 1)):
        w = mask_ref[layer].astype(jnp.float32)
        outs[side][spec, 0] = w
        for which in range(2):
            for k in range(spec):
                outs[2 * which + side][k, 0] = starts_ref[which, k, layer] * w


def coarse_fields_kernel(mask_ref, label_ref, rate_ref, out_ref):
    tile, ny, nz = mask_ref.shape
    half = tile // 2
    pores = mask_ref[...].astype(jnp.float32)
    source = pores * kappa_of(label_ref[...], rate_ref)
    for n, value in enumerate((pores, source)):
        pair = value.reshape(half, 2, ny, nz)
        pair = (pair[:, 0] + pair[:, 1]).reshape(half * ny, nz)
        for g, part in enumerate(fold(pair)):
            out_ref[n * half : n * half + half, :, g * 128 : g * 128 + 128] = part.reshape(half, ny // 2, 128)


def fold_all(layer, spec, tile, ny, nz):
    pair = [layer(k, 2 * i) + layer(k, 2 * i + 1) for k in range(spec) for i in range(tile // 2)]
    for g, part in enumerate(fold(jnp.concatenate(pair, axis=0))):
        yield slice(g * 128, g * 128 + 128), part.reshape(spec, tile // 2, ny // 2, 128)


def restrict_starts_kernel(starts_ref, out_ref, elo_ref, ehi_ref):
    count, spec, tile, ny, nz = starts_ref.shape
    for n in range(count):
        for lanes, part in fold_all(lambda k, i: starts_ref[n, k, i], spec, tile, ny, nz):
            out_ref[n, :, :, :, lanes] = part
            elo_ref[n, :, :, :, lanes] = part[:, :1]
            ehi_ref[n, :, :, :, lanes] = part[:, -1:]


def advance_kernel(which, starts_ref, mask_ref, u_ref, prev_ref, out_ref, *edges):
    _, spec, tile, ny, nz = starts_ref.shape

    def layer(k, i):
        return jnp.where(mask_ref[i] != 0, u_ref[k, i], starts_ref[which, k, i])

    for lanes, part in fold_all(layer, spec, tile, ny, nz):
        part = part - prev_ref[:, :, :, lanes]
        out_ref[:, :, :, lanes] = part
        if edges:
            edges[0][:, :, :, lanes] = part[:, :1]
            edges[1][:, :, :, lanes] = part[:, -1:]


def fine_kernel(
    first, u_ref, lo_ref, hi_ref, mask_ref, wlo_ref, whi_ref, label_ref,
    rate_ref, d_ref, st_ref, out_ref, elo_ref, ehi_ref, w_s, wide_s, src_s,
):
    tile = mask_ref.shape[0]
    spec = out_ref.shape[0]

    def cell(k, i):
        if i < 0:
            return lo_ref[k, 0]
        if i >= tile:
            return hi_ref[k, 0]
        if first is not None:
            return u_ref[first, k, i] * w_s[i]
        return u_ref[k, i]

    for i in range(tile):
        w_s[i] = mask_ref[i].astype(jnp.float32)
    for i in range(tile):
        below = w_s[i - 1] if i else wlo_ref[spec, 0]
        above = w_s[i + 1] if i + 1 < tile else whi_ref[spec, 0]
        wide_s[i] = w_s[i] * (plane_sum(w_s[i]) + below + above)
        source = w_s[i] * kappa_of(label_ref[i], rate_ref)
        src_s[i] = source * (1.0 - cell(0, i) * cell(1, i))

    def body(k, carry):
        d = d_ref[k]
        st = st_ref[k]
        for i in range(tile):
            c = cell(k, i)
            total = plane_sum(c) + cell(k, i - 1) + cell(k, i + 1)
            new = c + d * (w_s[i] * total - wide_s[i] * c) + st * src_s[i]
            out_ref[k, i] = new
            if i == 0:
                elo_ref[k, 0] = new
            if i == tile - 1:
                ehi_ref[k, 0] = new
        return carry

    lax.fori_loop(0, spec, body, 0)


def coarse_step(cell, por, src, d_ref, st_ref, spec, layers, emit):
    for i in layers:
        p = por(i)
        wide = p * (plane_sum(p) + por(i - 1) + por(i + 1))
        below, above = por(i - 1), por(i + 1)
        rate = float(SUBSTEPS) * (src(i) * (1.0 - cell(0, i) * cell(1, i)))
        for k in range(spec):
            c = cell(k, i)
            total = plane_sum(p * c) + below * cell(k, i - 1) + above * cell(k, i + 1)
            emit(k, i, c + d_ref[k] * (p * total - wide * c) + st_ref[k] * rate)


def section_kernel(
    received, q1lo, q1, q1hi, q2, prev1, prev2, flo, f, fhi, gate_ref, d_ref, st_ref, *refs
):
    parts = refs[: 3 * received]
    next_ref, d1_ref, d2_ref, start, mid = refs[3 * received :]
    spec = q1.shape[0]
    for side in range(3):
        value = jnp.zeros(q1.shape, jnp.float32)
        for part in parts[side::3]:
            value = value + part[...]
        start[:, 2 * side : 2 * side + 2] = value
    gate = gate_ref[0]

    def por(i):
        return flo[i + 2] if i < 0 else (f[i] if i < 2 else fhi[i - 2])

    def src(i):
        return flo[i + 4] if i < 0 else (f[i + 2] if i < 2 else fhi[i])

    def q(k, i):
        return q1lo[k, 0] if i < 0 else (q1[k, i] if i < 2 else q1hi[k, 0])

    def first(k, i, g):
        g = gate * g
        mid[k, i + 1] = g + q(k, i)
        if 0 <= i < 2:
            d1_ref[k, i] = g - prev1[k, i]

    coarse_step(lambda k, i: start[k, i + 2], por, src, d_ref, st_ref, spec, (-1, 0, 1, 2), first)

    def second(k, i, g):
        next_ref[k, i] = g + q2[k, i]
        d2_ref[k, i] = g - prev2[k, i]

    coarse_step(lambda k, i: mid[k, i + 1], por, src, d_ref, st_ref, spec, (0, 1), second)


def prev_kernel(lo, own, hi, flo, f, fhi, gate_ref, d_ref, st_ref, *outs):
    spec = own.shape[1]

    def por(i):
        return flo[1] if i < 0 else (f[i] if i < 2 else fhi[0])

    for n, out_ref in enumerate(outs):

        def cell(k, i):
            return lo[n, k, 0] if i < 0 else (own[n, k, i] if i < 2 else hi[n, k, 0])

        def emit(k, i, g):
            out_ref[k, i] = gate_ref[0] * g if n == 0 else g

        coarse_step(cell, por, lambda i: f[i + 2], d_ref, st_ref, spec, (0, 1), emit)


def final_kernel(starts_ref, mask_ref, ua_ref, ub_ref, da_ref, db_ref, out_ref):
    _, tile, ny, nz = starts_ref.shape
    spec, half, cy, cz = da_ref.shape
    which = pl.program_id(0)

    def write(u_ref, delta_ref):
        for g, part in enumerate(spread(delta_ref[...].reshape(spec * half * cy, cz))):
            part = part.reshape(spec, half, ny, 256)
            lanes = slice(g * 256, g * 256 + 256)
            for i in range(tile):
                keep = (mask_ref[i, :, lanes] != 0)[None]
                fine = jnp.where(keep, u_ref[:, i, :, lanes], starts_ref[:, i, :, lanes])
                out_ref[:, i, :, lanes] = part[:, i // 2] + fine

    @pl.when(which == 0)
    def _():
        write(ua_ref, da_ref)

    @pl.when(which == 1)
    def _():
        write(ub_ref, db_ref)


def final(starts, mask, ua, ub, da, db):
    count, spec, tile, ny, nz = starts.shape
    a = lambda n, k: (jnp.where(n == 0, k, 1), 0, 0, 0)
    b = lambda n, k: (jnp.where(n == 0, 0, k), 0, 0, 0)
    fine = (spec // 2, tile, ny, nz)
    coarse = (spec // 2,) + da.shape[1:]
    return pl.pallas_call(
        final_kernel,
        grid=(count, 2),
        out_shape=jax.ShapeDtypeStruct(starts.shape, jnp.float32),
        in_specs=[
            pl.BlockSpec((None,) + fine, lambda n, k: (n, k, 0, 0, 0)),
            pl.BlockSpec((tile, ny, nz), lambda n, k: (0, 0, 0)),
            pl.BlockSpec(fine, a),
            pl.BlockSpec(fine, b),
            pl.BlockSpec(coarse, a),
            pl.BlockSpec(coarse, b),
        ],
        out_specs=pl.BlockSpec((None,) + fine, lambda n, k: (n, k, 0, 0, 0)),
        compiler_params=pltpu.CompilerParams(vmem_limit_bytes=32 << 20),
        cost_estimate=pl.CostEstimate(flops=4 * starts.size, bytes_accessed=12 * starts.size, transcendentals=0),
    )(starts, mask, ua, ub, da, db)


def around(low_part, high_part):
    count = lax.axis_size("space")
    up = [(i, (i + 1) % count) for i in range(count)]
    down = [(target, source) for source, target in up]
    return lax.ppermute(high_part, "space", up), lax.ppermute(low_part, "space", down)


def local(starts, mask, label, diffusivity, stoich, rate):
    _, spec, tile, ny, nz = starts.shape
    edge = (spec, 1, ny, nz)
    edge_more = (spec + 1, 1, ny, nz)
    state = (spec, tile, ny, nz)
    coarse = (spec, tile // 2, ny // 2, nz // 2)
    coarse_edge = (spec, 1) + coarse[2:]
    place = lax.axis_index("tm")
    gate = jnp.where(place == 0, 0.0, 1.0).astype(jnp.float32).reshape(1)

    ea_lo, ea_hi, eb_lo, eb_hi = call(
        edge_kernel, [edge_more] * 2 + [edge] * 2, [VMEM] * 2, (starts, mask), 1 << 20
    )
    halo = [around(ea_lo, ea_hi), around(eb_lo, eb_hi)]
    wb, wa = halo[0]
    fields = call(
        coarse_fields_kernel, [(tile,) + coarse[2:]], [VMEM, VMEM, SMEM], (mask, label, rate), 1 << 26
    )[0]
    f_lo, f_hi = around(fields, fields)
    rs, r_lo, r_hi = call(
        restrict_starts_kernel, [(2,) + coarse] + [(2,) + coarse_edge] * 2, [VMEM], (starts,), 1 << 29
    )
    r_lo, r_hi = around(r_lo, r_hi)

    states = [starts, starts]
    for turn in range(SUBSTEPS):
        for n in range(2):
            below, above = halo[n]
            args = (states[n], below, above, mask, wb, wa, label, rate, diffusivity, stoich)
            first = n if turn == 0 else None
            shapes = [jax.ShapeDtypeStruct(x, jnp.float32) for x in (state, edge, edge)]
            states[n], e_lo, e_hi = pl.pallas_call(
                functools.partial(fine_kernel, first),
                out_shape=shapes,
                in_specs=[VMEM] * 7 + [SMEM] * 3,
                out_specs=[VMEM] * 3,
                scratch_shapes=[pltpu.VMEM((tile, ny, nz), jnp.float32)] * 3,
                compiler_params=pltpu.CompilerParams(vmem_limit_bytes=32 << 20),
                cost_estimate=pl.CostEstimate(flops=1 << 24, bytes_accessed=6 << 20, transcendentals=0),
            )(*args)
            if turn + 1 < SUBSTEPS:
                halo[n] = around(e_lo, e_hi)
    prev = call(
        prev_kernel, [coarse] * 2, [VMEM] * 6 + [SMEM] * 3,
        (r_lo, rs, r_hi, f_lo, fields, f_hi, gate, diffusivity, stoich), 1 << 23,
    )
    q1, q_lo, q_hi = call(
        functools.partial(advance_kernel, 0), [coarse] + [coarse_edge] * 2, [VMEM] * 4,
        (starts, mask, states[0], prev[0]), 1 << 28,
    )
    q_lo, q_hi = around(q_lo, q_hi)
    q2 = call(
        functools.partial(advance_kernel, 1), [coarse], [VMEM] * 4,
        (starts, mask, states[1], prev[1]), 1 << 28,
    )[0]

    def section(parts):
        return pl.pallas_call(
            functools.partial(section_kernel, len(parts) // 3),
            out_shape=[jax.ShapeDtypeStruct(coarse, jnp.float32)] * 3,
            in_specs=[VMEM] * 9 + [SMEM] * 3 + [VMEM] * len(parts),
            out_specs=[VMEM] * 3,
            scratch_shapes=[
                pltpu.VMEM((spec, 6) + coarse[2:], jnp.float32),
                pltpu.VMEM((spec, 4) + coarse[2:], jnp.float32),
            ],
            compiler_params=pltpu.CompilerParams(vmem_limit_bytes=32 << 20),
            cost_estimate=pl.CostEstimate(flops=1 << 22, bytes_accessed=2 << 20, transcendentals=0),
        )(q_lo, q1, q_hi, q2, prev[0], prev[1], f_lo, fields, f_hi, gate, diffusivity, stoich, *parts)

    sections = lax.axis_size("tm")
    count = lax.axis_size("space")
    parts = []
    for target in range(1, sections):
        out = section(parts)[0]
        base, there = (target - 1) * count, target * count
        for step in (1, 0, -1):
            pairs = [(base + i, there + (i + step) % count) for i in range(count)]
            parts.append(lax.ppermute(out, ("tm", "space"), pairs))
    _, delta_a, delta_b = section(parts)
    return final(starts, mask, states[0], states[1], delta_a, delta_b)


def solution(mesh):
    placed = (
        P("tm", None, "space", None, None),
        P("space", None, None),
        P("space", None, None),
        P(),
        P(),
        P(),
    )
    return jax.shard_map(
        local,
        mesh=mesh,
        in_specs=placed,
        out_specs=P("tm", None, "space", None, None),
        check_vma=False,
    )
```

time: 226 us -> 198 us (0.88)
  Pallas kernels: 77.8 us -> 57.7 us
  other arithmetic: 8.95 us -> 0 us
  waiting for transfers between devices: 77.6 us -> 84.5 us
  local copies, waits for them, and re-layouts: 12.1 us -> 7.04 us
    pallas_call x5, Pallas kernels: 27.6 us -> 11.7 us  [the longest x4 8.06 us: section(): pl.pallas_call(functools.partial(section_kernel, len(parts) // 3), out_sh...]
    ppermute x14 -> x11, starting transfers between devices: 6.52 us -> 16.3 us  [around(): lax.ppermute(high_part, 'space', up)]
    ppermute x14 -> x11, starting transfers between devices: 30.5 us -> 20.9 us  [around(): lax.ppermute(low_part, 'space', down)]
    ppermute x14 -> x11, waiting for transfers between devices: 9.33 us -> 18.8 us  [around(): lax.ppermute(low_part, 'space', down)]
    add x9 -> x0, other arithmetic: 6.76 us -> none  [local(): current[slot] = current[slot] + lax.ppermute(out, ('tm', 'space'), pairs)]
    pallas_call x8 -> x6, Pallas kernels: 23.7 us -> 17.3 us  [call(): pl.pallas_call(kernel, out_shape=shapes, in_specs=specs, out_specs=[VMEM]...]
    unnamed x92 -> x28, local copies, waits for them, and re-layouts: 11.3 us -> 7.04 us
    ppermute x14 -> x11, waiting for transfers between devices: 26.3 us -> 22.2 us  [around(): lax.ppermute(high_part, 'space', up)]
  transfers between devices with their start and end apart: 37 -> 31, of which waited for: 10 -> 16; matrix products, arithmetic and copies ran while one was open for 3% -> 0% of each run, Pallas kernels for 21% -> 22%
where the time goes in v2:
time: 198 us; the launch traced here: 197 us
  waiting for transfers between devices  84.5 us (43%)
  Pallas kernels  57.7 us (29%)
  starting transfers between devices  47 us (24%)
  local copies, waits for them, and re-layouts  7.04 us (4%)
    ppermute x9, waiting for transfers between devices, local(): parts.append(lax.ppermute(out, ('tm', 'space'), pairs))  43.5 us
    pallas_call x8, Pallas kernels, local(): pl.pallas_call(functools.partial(fine_kernel, first), out_shape=shapes, i...  28.7 us
    ppermute x11, waiting for transfers between devices, around(): lax.ppermute(high_part, 'space', up)  22.2 us
    ppermute x11, starting transfers between devices, around(): lax.ppermute(low_part, 'space', down)  20.9 us
    ppermute x11, waiting for transfers between devices, around(): lax.ppermute(low_part, 'space', down)  18.8 us
    pallas_call x6, Pallas kernels, call(): pl.pallas_call(kernel, out_shape=shapes, in_specs=specs, out_specs=[VMEM]...  17.3 us
    ppermute x11, starting transfers between devices, around(): lax.ppermute(high_part, 'space', up)  16.3 us
    ppermute x9, starting transfers between devices, local(): parts.append(lax.ppermute(out, ('tm', 'space'), pairs))  9.79 us
  transfers between devices with their start and end apart: 31, of which 16 were waited for; matrix products, arithmetic and copies ran while one was open for 0% of the time, Pallas kernels for 22%

profile of v2, /device:TPU:4, one launch (start us, length us, event | category | flops | bytes accessed | tf_op | source)
XLA Modules:
  0.0 196.5 jit_solution(5342815126405330427)
XLA Ops:
  1.1 2.6 %shard_map.64 = (f32[9,1,16,1024]{3,2,1,0:T(8,128)S(1)}, f32[9,1,16,1024]{3,2,1,0:T(8,128)S(1)}, f32[8,1,16,1024]{3,2,1,0:T(8,128)S(1)}, f32[8,1,16,1024]{3,2,1,0:T(8,128)S(1)}) custom-call(f32[2,8,4,16,1024]{4,3,2,1,0:T(8,128)} %starts_ref.9, s32[4,16,1024]{2,1,0:T(8,128)S(1)} %copy-done.2), custom_call_target="tpu_custom_call" | custom-call | flops 1048576 | bytes 6684672 | tf_op jit(solution)/shard_map/pallas_call | solution.py:19
  3.8 3.5 %collective-permute-start.1 = (f32[9,1,16,1024]{3,2,1,0:T(8,128)S(1)}, f32[9,1,16,1024]{3,2,1,0:T(8,128)S(1)}, u32[]{:S(2)}, u32[]{:S(2)}) collective-permute-start(f32[9,1,16,1024]{3,2,1,0:T(8,128)S(1)} %get-tuple-element.43), channel_id=1, source_target_pairs={{1,0},{2,1},{3,2},{4,3},{5,4},{6,5},{7,6},{0,7},{9,8},{10,9},{11,1... | collective-permute-start | bytes 1769480 | tf_op jit(solution)/shard_map/ppermute | solution.py:295
  7.3 3.5 %collective-permute-start.9 = (f32[8,1,16,1024]{3,2,1,0:T(8,128)S(1)}, f32[8,1,16,1024]{3,2,1,0:T(8,128)S(1)}, u32[]{:S(2)}, u32[]{:S(2)}) collective-permute-start(f32[8,1,16,1024]{3,2,1,0:T(8,128)S(1)} %get-tuple-element.55), channel_id=1, source_target_pairs={{1,0},{2,1},{3,2},{4,3},{5,4},{6,5},{7,6},{0,7},{9,8},{10,9},{11,1... | collective-permute-start | bytes 1572872 | tf_op jit(solution)/shard_map/ppermute | solution.py:295
  10.8 8.2 %collective-permute-done.lo_ref.wlo_ref = f32[9,1,16,1024]{3,2,1,0:T(8,128)S(1)} collective-permute-done((f32[9,1,16,1024]{3,2,1,0:T(8,128)S(1)}, f32[9,1,16,1024]{3,2,1,0:T(8,128)S(1)}, u32[]{:S(2)}, u32[]{:S(2)}) %collective-permute-start) | collective-permute-done | bytes 589856 | tf_op jit(solution)/shard_map/ppermute | solution.py:295
  19.0 2.1 %collective-permute-done.1.hi_ref.whi_ref = f32[9,1,16,1024]{3,2,1,0:T(8,128)S(1)} collective-permute-done((f32[9,1,16,1024]{3,2,1,0:T(8,128)S(1)}, f32[9,1,16,1024]{3,2,1,0:T(8,128)S(1)}, u32[]{:S(2)}, u32[]{:S(2)}) %collective-permute-start.1) | collective-permute-done | bytes 589856 | tf_op jit(solution)/shard_map/ppermute | solution.py:295
  21.1 2.8 %shard_map.65 = (f32[8,4,16,1024]{3,2,1,0:T(8,128)S(1)}, f32[8,1,16,1024]{3,2,1,0:T(8,128)S(1)}, f32[8,1,16,1024]{3,2,1,0:T(8,128)S(1)}) custom-call(f32[2,8,4,16,1024]{4,3,2,1,0:T(8,128)S(1)} %copy-done, f32[9,1,16,1024]{3,2,1,0:T(8,128)S(1)} %collective-permute-done.lo_ref.wlo_ref, f32[9,1,16,1024]{3,2,1,0:T(8,128)S(1)} %collective-permute-done.1.hi_ref.whi_ref, ...), custom_call_target="tpu_custom_call" | custom-call | flops 16777216 | bytes 6291456 | tf_op jit(solution)/shard_map/pallas_call | solution.py:329
  24.0 2.4 %collective-permute-start.2 = (f32[8,1,16,1024]{3,2,1,0:T(8,128)S(1)}, f32[8,1,16,1024]{3,2,1,0:T(8,128)S(1)}, u32[]{:S(2)}, u32[]{:S(2)}) collective-permute-start(f32[8,1,16,1024]{3,2,1,0:T(8,128)S(1)} %get-tuple-element.45), channel_id=1, source_target_pairs={{0,1},{1,2},{2,3},{3,4},{4,5},{5,6},{6,7},{7,0},{8,9},{9,10},{10,1... | collective-permute-start | bytes 1572872 | tf_op jit(solution)/shard_map/ppermute | solution.py:295
  26.4 1.4 collective-permute-start.3
  27.8 2.5 %collective-permute-done.8.lo_ref = f32[8,1,16,1024]{3,2,1,0:T(8,128)S(1)} collective-permute-done((f32[8,1,16,1024]{3,2,1,0:T(8,128)S(1)}, f32[8,1,16,1024]{3,2,1,0:T(8,128)S(1)}, u32[]{:S(2)}, u32[]{:S(2)}) %collective-permute-start.8) | collective-permute-done | bytes 524320 | tf_op jit(solution)/shard_map/ppermute | solution.py:295
  30.2 2.1 %collective-permute-done.9.hi_ref = f32[8,1,16,1024]{3,2,1,0:T(8,128)S(1)} collective-permute-done((f32[8,1,16,1024]{3,2,1,0:T(8,128)S(1)}, f32[8,1,16,1024]{3,2,1,0:T(8,128)S(1)}, u32[]{:S(2)}, u32[]{:S(2)}) %collective-permute-start.9) | collective-permute-done | bytes 524320 | tf_op jit(solution)/shard_map/ppermute | solution.py:295
  32.3 2.9 %shard_map.69 = (f32[8,4,16,1024]{3,2,1,0:T(8,128)S(1)}, f32[8,1,16,1024]{3,2,1,0:T(8,128)S(1)}, f32[8,1,16,1024]{3,2,1,0:T(8,128)S(1)}) custom-call(f32[2,8,4,16,1024]{4,3,2,1,0:T(8,128)S(1)} %copy-done, f32[8,1,16,1024]{3,2,1,0:T(8,128)S(1)} %collective-permute-done.8.lo_ref, f32[8,1,16,1024]{3,2,1,0:T(8,128)S(1)} %collective-permute-done.9.hi_ref, ...), custom_call_target="tpu_custom_call" | custom-call | flops 16777216 | bytes 6291456 | tf_op jit(solution)/shard_map/pallas_call | solution.py:329
  35.2 2.4 %collective-permute-start.10 = (f32[8,1,16,1024]{3,2,1,0:T(8,128)S(1)}, f32[8,1,16,1024]{3,2,1,0:T(8,128)S(1)}, u32[]{:S(2)}, u32[]{:S(2)}) collective-permute-start(f32[8,1,16,1024]{3,2,1,0:T(8,128)S(1)} %get-tuple-element.57), channel_id=1, source_target_pairs={{0,1},{1,2},{2,3},{3,4},{4,5},{5,6},{6,7},{7,0},{8,9},{9,10},{10,1... | collective-permute-start | bytes 1572872 | tf_op jit(solution)/shard_map/ppermute | solution.py:295
  37.7 1.4 collective-permute-start.11
  39.1 2.4 %collective-permute-done.2.lo_ref = f32[8,1,16,1024]{3,2,1,0:T(8,128)S(1)} collective-permute-done((f32[8,1,16,1024]{3,2,1,0:T(8,128)S(1)}, f32[8,1,16,1024]{3,2,1,0:T(8,128)S(1)}, u32[]{:S(2)}, u32[]{:S(2)}) %collective-permute-start.2) | collective-permute-done | bytes 524320 | tf_op jit(solution)/shard_map/ppermute | solution.py:295
  41.5 2.1 %collective-permute-done.3.hi_ref = f32[8,1,16,1024]{3,2,1,0:T(8,128)S(1)} collective-permute-done((f32[8,1,16,1024]{3,2,1,0:T(8,128)S(1)}, f32[8,1,16,1024]{3,2,1,0:T(8,128)S(1)}, u32[]{:S(2)}, u32[]{:S(2)}) %collective-permute-start.3) | collective-permute-done | bytes 524320 | tf_op jit(solution)/shard_map/ppermute | solution.py:295
  43.6 3.8 %shard_map.66 = (f32[8,4,16,1024]{3,2,1,0:T(8,128)S(1)}, f32[8,1,16,1024]{3,2,1,0:T(8,128)S(1)}, f32[8,1,16,1024]{3,2,1,0:T(8,128)}) custom-call(f32[8,4,16,1024]{3,2,1,0:T(8,128)S(1)} %get-tuple-element.44.u_ref, f32[8,1,16,1024]{3,2,1,0:T(8,128)S(1)} %collective-permute-done.2.lo_ref, f32[8,1,16,1024]{3,2,1,0:T(8,128)S(1)} %collective-permute-done.3.hi_ref, ...), custom_call_target="tpu_custom_call" | custom-call | flops 16777216 | bytes 6291456 | tf_op jit(solution)/shard_map/pallas_call | solution.py:329
  47.3 2.4 %collective-permute-start.4 = (f32[8,1,16,1024]{3,2,1,0:T(8,128)}, f32[8,1,16,1024]{3,2,1,0:T(8,128)S(1)}, u32[]{:S(2)}, u32[]{:S(2)}) collective-permute-start(f32[8,1,16,1024]{3,2,1,0:T(8,128)} %get-tuple-element.48), channel_id=1, source_target_pairs={{0,1},{1,2},{2,3},{3,4},{4,5},{5,6},{6,7},{7,0},{8,9},{9,10},{10,1... | collective-permute-start | bytes 1572872 | tf_op jit(solution)/shard_map/ppermute | solution.py:295
  49.7 1.3 collective-permute-start.5
  51.1 1.7 collective-permute-done.10.lo_ref
  54.0 3.8 %shard_map.70 = (f32[8,4,16,1024]{3,2,1,0:T(8,128)S(1)}, f32[8,1,16,1024]{3,2,1,0:T(8,128)}, f32[8,1,16,1024]{3,2,1,0:T(8,128)}) custom-call(f32[8,4,16,1024]{3,2,1,0:T(8,128)S(1)} %get-tuple-element.56.u_ref, f32[8,1,16,1024]{3,2,1,0:T(8,128)S(1)} %collective-permute-done.10.lo_ref, f32[8,1,16,1024]{3,2,1,0:T(8,128)S(1)} %collective-permute-done.11.hi_ref, ...), custom_call_target="tpu_custom_call" | custom-call | flops 16777216 | bytes 6291456 | tf_op jit(solution)/shard_map/pallas_call | solution.py:329
  57.8 3.2 %collective-permute-start.12 = (f32[8,1,16,1024]{3,2,1,0:T(8,128)}, f32[8,1,16,1024]{3,2,1,0:T(8,128)S(1)}, u32[]{:S(2)}, u32[]{:S(2)}) collective-permute-start(f32[8,1,16,1024]{3,2,1,0:T(8,128)} %get-tuple-element.60), channel_id=1, source_target_pairs={{0,1},{1,2},{2,3},{3,4},{4,5},{5,6},{6,7},{7,0},{8,9},{9,10},{10,1... | collective-permute-start | bytes 1572872 | tf_op jit(solution)/shard_map/ppermute | solution.py:295
  61.5 3.6 %shard_map.73 = (f32[2,8,2,8,512]{4,3,2,1,0:T(8,128)S(1)}, f32[2,8,1,8,512]{4,3,2,1,0:T(8,128)}, f32[2,8,1,8,512]{4,3,2,1,0:T(8,128)S(1)}) custom-call(f32[2,8,4,16,1024]{4,3,2,1,0:T(8,128)S(1)} %copy-done), custom_call_target="tpu_custom_call" | custom-call | flops 536870912 | bytes 5242880 | tf_op jit(solution)/shard_map/pallas_call | solution.py:19
  65.2 3.5 %shard_map.67 = (f32[8,4,16,1024]{3,2,1,0:T(8,128)S(1)}, f32[8,1,16,1024]{3,2,1,0:T(8,128)}, f32[8,1,16,1024]{3,2,1,0:T(8,128)}) custom-call(f32[8,4,16,1024]{3,2,1,0:T(8,128)S(1)} %get-tuple-element.47.u_ref, f32[8,1,16,1024]{3,2,1,0:T(8,128)S(1)} %collective-permute-done.4.lo_ref, f32[8,1,16,1024]{3,2,1,0:T(8,128)S(1)} %collective-permute-done.5.hi_ref, ...), custom_call_target="tpu_custom_call" | custom-call | flops 16777216 | bytes 6291456 | tf_op jit(solution)/shard_map/pallas_call | solution.py:329
  70.1 3.2 %collective-permute-start.6 = (f32[8,1,16,1024]{3,2,1,0:T(8,128)}, f32[8,1,16,1024]{3,2,1,0:T(8,128)S(1)}, u32[]{:S(2)}, u32[]{:S(2)}) collective-permute-start(f32[8,1,16,1024]{3,2,1,0:T(8,128)} %get-tuple-element.51), channel_id=1, source_target_pairs={{0,1},{1,2},{2,3},{3,4},{4,5},{5,6},{6,7},{7,0},{8,9},{9,10},{10,1... | collective-permute-start | bytes 1572872 | tf_op jit(solution)/shard_map/ppermute | solution.py:295
  73.8 1.9 shard_map.74.f
  76.6 3.6 %collective-permute-start.19 = (f32[4,8,512]{2,1,0:T(8,128)S(1)}, f32[4,8,512]{2,1,0:T(8,128)S(1)}, u32[]{:S(2)}, u32[]{:S(2)}) collective-permute-start(f32[4,8,512]{2,1,0:T(8,128)S(1)} %shard_map.74.f), channel_id=1, source_target_pairs={{1,0},{2,1},{3,2},{4,3},{5,4},{6,5},{7,6},{0,7},{9,8},{10,9},{11,1... | collective-permute-start | bytes 196616 | tf_op jit(solution)/shard_map/ppermute | solution.py:295
  80.2 3.8 %shard_map.71 = (f32[8,4,16,1024]{3,2,1,0:T(8,128)S(1)}, f32[8,1,16,1024]{3,2,1,0:T(8,128)}, f32[8,1,16,1024]{3,2,1,0:T(8,128)}) custom-call(f32[8,4,16,1024]{3,2,1,0:T(8,128)S(1)} %get-tuple-element.59.u_ref, f32[8,1,16,1024]{3,2,1,0:T(8,128)S(1)} %collective-permute-done.12.lo_ref, f32[8,1,16,1024]{3,2,1,0:T(8,128)S(1)} %collective-permute-done.13.hi_ref, ...), custom_call_target="tpu_custom_call" | custom-call | flops 16777216 | bytes 6291456 | tf_op jit(solution)/shard_map/pallas_call | solution.py:329
  84.0 1.3 copy-done.7
  85.3 7.5 %collective-permute-done.18.flo = f32[4,8,512]{2,1,0:T(8,128)S(1)} collective-permute-done((f32[4,8,512]{2,1,0:T(8,128)S(1)}, f32[4,8,512]{2,1,0:T(8,128)S(1)}, u32[]{:S(2)}, u32[]{:S(2)}) %collective-permute-start.18) | collective-permute-done | bytes 65568 | tf_op jit(solution)/shard_map/ppermute | solution.py:295
  92.8 3.5 %collective-permute-start.15 = (f32[8,1,16,1024]{3,2,1,0:T(8,128)}, f32[8,1,16,1024]{3,2,1,0:T(8,128)}, u32[]{:S(2)}, u32[]{:S(2)}) collective-permute-start(f32[8,1,16,1024]{3,2,1,0:T(8,128)} %get-tuple-element.64), channel_id=1, source_target_pairs={{1,0},{2,1},{3,2},{4,3},{5,4},{6,5},{7,6},{0,7},{9,8},{10,9},{11,1... | collective-permute-start | bytes 1572872 | tf_op jit(solution)/shard_map/ppermute | solution.py:295
  97.1 10.4 %collective-permute-done.17.hi = f32[2,8,1,8,512]{4,3,2,1,0:T(8,128)} collective-permute-done((f32[2,8,1,8,512]{4,3,2,1,0:T(8,128)}, f32[2,8,1,8,512]{4,3,2,1,0:T(8,128)}, u32[]{:S(2)}, u32[]{:S(2)}) %collective-permute-start.17) | collective-permute-done | bytes 262176 | tf_op jit(solution)/shard_map/ppermute | solution.py:295
  108.4 1.4 shard_map.75
  109.9 1.6 copy-done.6
  111.5 3.8 %shard_map.68 = (f32[8,4,16,1024]{3,2,1,0:T(8,128)S(1)}, f32[8,1,16,1024]{3,2,1,0:T(8,128)}, f32[8,1,16,1024]{3,2,1,0:T(8,128)}) custom-call(f32[8,4,16,1024]{3,2,1,0:T(8,128)S(1)} %copy-done.6, f32[8,1,16,1024]{3,2,1,0:T(8,128)S(1)} %collective-permute-done.6.lo_ref, f32[8,1,16,1024]{3,2,1,0:T(8,128)S(1)} %collective-permute-done.7.hi_ref, ...), custom_call_target="tpu_custom_call" | custom-call | flops 16777216 | bytes 6291456 | tf_op jit(solution)/shard_map/pallas_call | solution.py:329
  115.3 3.9 %shard_map.76 = (f32[8,2,8,512]{3,2,1,0:T(8,128)S(1)}, f32[8,1,8,512]{3,2,1,0:T(8,128)S(1)}, f32[8,1,8,512]{3,2,1,0:T(8,128)S(1)}) custom-call(f32[2,8,4,16,1024]{4,3,2,1,0:T(8,128)} %starts_ref.9, s32[4,16,1024]{2,1,0:T(8,128)S(1)} %copy-done.3, f32[8,4,16,1024]{3,2,1,0:T(8,128)S(1)} %get-tuple-element.53.u_ref.ua_ref, ...), custom_call_target="tpu_custom_call" | custom-call | flops 268435456 | bytes 7340032 | tf_op jit(solution)/shard_map/pallas_call | solution.py:19
  119.2 2.6 %collective-permute-start.20 = (f32[8,1,8,512]{3,2,1,0:T(8,128)S(1)}, f32[8,1,8,512]{3,2,1,0:T(8,128)S(1)}, u32[]{:S(2)}, u32[]{:S(2)}) collective-permute-start(f32[8,1,8,512]{3,2,1,0:T(8,128)S(1)} %get-tuple-element.70), channel_id=1, source_target_pairs={{0,1},{1,2},{2,3},{3,4},{4,5},{5,6},{6,7},{7,0},{8,9},{9,10},{10,1... | collective-permute-start | bytes 393224 | tf_op jit(solution)/shard_map/ppermute | solution.py:295
  121.8 1.5 collective-permute-start.21
  123.4 4.2 %shard_map.72 = (f32[8,4,16,1024]{3,2,1,0:T(8,128)S(1)}, f32[8,1,16,1024]{3,2,1,0:T(8,128)}, f32[8,1,16,1024]{3,2,1,0:T(8,128)}) custom-call(f32[8,4,16,1024]{3,2,1,0:T(8,128)S(1)} %copy-done.8, f32[8,1,16,1024]{3,2,1,0:T(8,128)} %collective-permute-done.14.lo_ref, f32[8,1,16,1024]{3,2,1,0:T(8,128)} %collective-permute-done.15.hi_ref, ...), custom_call_target="tpu_custom_call" | custom-call | flops 16777216 | bytes 6291456 | tf_op jit(solution)/shard_map/pallas_call | solution.py:329
  127.6 3.8 %shard_map.77.q2 = f32[8,2,8,512]{3,2,1,0:T(8,128)S(1)} custom-call(f32[2,8,4,16,1024]{4,3,2,1,0:T(8,128)} %starts_ref.9, s32[4,16,1024]{2,1,0:T(8,128)S(1)} %copy-done.3, f32[8,4,16,1024]{3,2,1,0:T(8,128)S(1)} %get-tuple-element.65.u_ref.ub_ref, f32[8,2,8,512]{3,2,1,0:T(8,128)S(1)} %get-tuple-element.73.prev_ref.prev2), custom_call_target="tpu_custom_call" | custom-call | flops 268435456 | bytes 7077888 | tf_op jit(solution)/shard_map/pallas_call | solution.py:19
  131.4 2.0 shard_map.78
  135.4 2.0 %shard_map.79 = (f32[8,2,8,512]{3,2,1,0:T(8,128)S(1)}, f32[8,2,8,512]{3,2,1,0:T(8,128)}, f32[8,2,8,512]{3,2,1,0:T(8,128)}) custom-call(f32[8,1,8,512]{3,2,1,0:T(8,128)S(1)} %collective-permute-done.20.q1lo, f32[8,2,8,512]{3,2,1,0:T(8,128)S(1)} %get-tuple-element.71.q1, f32[8,1,8,512]{3,2,1,0:T(8,128)S(1)} %collective-permute-done.21.q1hi, ...), custom_call_target="tpu_custom_call" | custom-call | flops 4194304 | bytes 2097152 | tf_op jit(solution)/shard_map/pallas_call | solution.py:355
  141.3 19.3 %collective-permute-done.25.refs_3_ = f32[8,2,8,512]{3,2,1,0:T(8,128)S(1)} collective-permute-done((f32[8,2,8,512]{3,2,1,0:T(8,128)S(1)}, f32[8,2,8,512]{3,2,1,0:T(8,128)S(1)}, u32[]{:S(2)}, u32[]{:S(2)}) %collective-permute-start.25) | collective-permute-done | bytes 262176 | tf_op jit(solution)/shard_map/ppermute | solution.py:376
  160.6 13.8 %collective-permute-done.26.refs_4_ = f32[8,2,8,512]{3,2,1,0:T(8,128)S(1)} collective-permute-done((f32[8,2,8,512]{3,2,1,0:T(8,128)S(1)}, f32[8,2,8,512]{3,2,1,0:T(8,128)S(1)}, u32[]{:S(2)}, u32[]{:S(2)}) %collective-permute-start.26) | collective-permute-done | bytes 262176 | tf_op jit(solution)/shard_map/ppermute | solution.py:376
  174.5 2.0 %shard_map.80 = (f32[8,2,8,512]{3,2,1,0:T(8,128)S(1)}, f32[8,2,8,512]{3,2,1,0:T(8,128)}, f32[8,2,8,512]{3,2,1,0:T(8,128)}) custom-call(f32[8,1,8,512]{3,2,1,0:T(8,128)S(1)} %collective-permute-done.20.q1lo, f32[8,2,8,512]{3,2,1,0:T(8,128)S(1)} %get-tuple-element.71.q1, f32[8,1,8,512]{3,2,1,0:T(8,128)S(1)} %collective-permute-done.21.q1hi, ...), custom_call_target="tpu_custom_call" | custom-call | flops 4194304 | bytes 2097152 | tf_op jit(solution)/shard_map/pallas_call | solution.py:355
  180.4 6.9 %collective-permute-done.28.refs_6_ = f32[8,2,8,512]{3,2,1,0:T(8,128)S(1)} collective-permute-done((f32[8,2,8,512]{3,2,1,0:T(8,128)S(1)}, f32[8,2,8,512]{3,2,1,0:T(8,128)S(1)}, u32[]{:S(2)}, u32[]{:S(2)}) %collective-permute-start.28) | collective-permute-done | bytes 262176 | tf_op jit(solution)/shard_map/ppermute | solution.py:376
  187.3 3.4 %collective-permute-done.29.refs_7_ = f32[8,2,8,512]{3,2,1,0:T(8,128)S(1)} collective-permute-done((f32[8,2,8,512]{3,2,1,0:T(8,128)S(1)}, f32[8,2,8,512]{3,2,1,0:T(8,128)S(1)}, u32[]{:S(2)}, u32[]{:S(2)}) %collective-permute-start.29) | collective-permute-done | bytes 262176 | tf_op jit(solution)/shard_map/ppermute | solution.py:376
  190.8 2.1 %shard_map.81 = (f32[8,2,8,512]{3,2,1,0:T(8,128)}, f32[8,2,8,512]{3,2,1,0:T(8,128)S(1)}, f32[8,2,8,512]{3,2,1,0:T(8,128)S(1)}) custom-call(f32[8,1,8,512]{3,2,1,0:T(8,128)S(1)} %collective-permute-done.20.q1lo, f32[8,2,8,512]{3,2,1,0:T(8,128)S(1)} %get-tuple-element.71.q1, f32[8,1,8,512]{3,2,1,0:T(8,128)S(1)} %collective-permute-done.21.q1hi, ...), custom_call_target="tpu_custom_call" | custom-call | flops 4194304 | bytes 2097152 | tf_op jit(solution)/shard_map/pallas_call | solution.py:355
  192.8 3.7 %shard_map.82 = f32[2,8,4,16,1024]{4,3,2,1,0:T(8,128)} custom-call(f32[2,8,4,16,1024]{4,3,2,1,0:T(8,128)S(1)} %copy-done.1, s32[4,16,1024]{2,1,0:T(8,128)S(1)} %copy-done.3, f32[8,4,16,1024]{3,2,1,0:T(8,128)S(1)} %get-tuple-element.53.u_ref.ua_ref, f32[8,4,16,1024]{3,2,1,0:T(8,128)S(1)} %get-tuple-element.65.u_ref.ub_ref, ...), custom_call_target="tpu_custom_call" | custom-call | flops 4194304 | bytes 12582912 | tf_op jit(solution)/shard_map/pallas_call | solution.py:273
  (61 shorter events, 17.2 us)
Async XLA Ops:
  0.0 21.1 %copy-start = (f32[2,8,4,16,1024]{4,3,2,1,0:T(8,128)S(1)}, f32[2,8,4,16,1024]{4,3,2,1,0:T(8,128)}, u32[]{:S(2)}) copy-start(f32[2,8,4,16,1024]{4,3,2,1,0:T(8,128)} %starts_ref.9) | copy-start | bytes 12582916
  0.0 1.1 copy-start.2
  1.1 20.0 %copy-start.4 = (s32[4,16,1024]{2,1,0:T(8,128)S(1)}, s32[4,16,1024]{2,1,0:T(8,128)}, u32[]{:S(2)}) copy-start(s32[4,16,1024]{2,1,0:T(8,128)} %label_ref.17) | copy-start | bytes 786436
  1.1 20.0 %copy-start.11 = (f32[8]{0:T(128)S(1)}, f32[8]{0:T(128)}, u32[]{:S(2)}) copy-start(f32[8]{0:T(128)} %d_ref.25) | copy-start | bytes 100
  1.1 20.0 %copy-start.12 = (f32[8]{0:T(128)S(1)}, f32[8]{0:T(128)}, u32[]{:S(2)}) copy-start(f32[8]{0:T(128)} %st_ref.25) | copy-start | bytes 100
  1.1 20.0 %copy-start.13 = (f32[4]{0:T(128)S(1)}, f32[4]{0:T(128)}, u32[]{:S(2)}) copy-start(f32[4]{0:T(128)} %rate_ref.17) | copy-start | bytes 52
  3.7 15.3 %collective-permute-start = (f32[9,1,16,1024]{3,2,1,0:T(8,128)S(1)}, f32[9,1,16,1024]{3,2,1,0:T(8,128)S(1)}, u32[]{:S(2)}, u32[]{:S(2)}) collective-permute-start(f32[9,1,16,1024]{3,2,1,0:T(8,128)S(1)} %get-tuple-element.42), channel_id=1, source_target_pairs={{0,1},{1,2},{2,3},{3,4},{4,5},{5,6},{6,7},{7,0},{8,9},{9,10},{10,1... | collective-permute-start | bytes 1769480 | tf_op jit(solution)/shard_map/ppermute | solution.py:295
  3.8 17.3 %collective-permute-start.1 = (f32[9,1,16,1024]{3,2,1,0:T(8,128)S(1)}, f32[9,1,16,1024]{3,2,1,0:T(8,128)S(1)}, u32[]{:S(2)}, u32[]{:S(2)}) collective-permute-start(f32[9,1,16,1024]{3,2,1,0:T(8,128)S(1)} %get-tuple-element.43), channel_id=1, source_target_pairs={{1,0},{2,1},{3,2},{4,3},{5,4},{6,5},{7,6},{0,7},{9,8},{10,9},{11,1... | collective-permute-start | bytes 1769480 | tf_op jit(solution)/shard_map/ppermute | solution.py:295
  7.3 22.9 %collective-permute-start.8 = (f32[8,1,16,1024]{3,2,1,0:T(8,128)S(1)}, f32[8,1,16,1024]{3,2,1,0:T(8,128)S(1)}, u32[]{:S(2)}, u32[]{:S(2)}) collective-permute-start(f32[8,1,16,1024]{3,2,1,0:T(8,128)S(1)} %get-tuple-element.54), channel_id=1, source_target_pairs={{0,1},{1,2},{2,3},{3,4},{4,5},{5,6},{6,7},{7,0},{8,9},{9,10},{10,1... | collective-permute-start | bytes 1572872 | tf_op jit(solution)/shard_map/ppermute | solution.py:295
  7.3 25.0 %collective-permute-start.9 = (f32[8,1,16,1024]{3,2,1,0:T(8,128)S(1)}, f32[8,1,16,1024]{3,2,1,0:T(8,128)S(1)}, u32[]{:S(2)}, u32[]{:S(2)}) collective-permute-start(f32[8,1,16,1024]{3,2,1,0:T(8,128)S(1)} %get-tuple-element.55), channel_id=1, source_target_pairs={{1,0},{2,1},{3,2},{4,3},{5,4},{6,5},{7,6},{0,7},{9,8},{10,9},{11,1... | collective-permute-start | bytes 1572872 | tf_op jit(solution)/shard_map/ppermute | solution.py:295
  24.0 17.5 %collective-permute-start.2 = (f32[8,1,16,1024]{3,2,1,0:T(8,128)S(1)}, f32[8,1,16,1024]{3,2,1,0:T(8,128)S(1)}, u32[]{:S(2)}, u32[]{:S(2)}) collective-permute-start(f32[8,1,16,1024]{3,2,1,0:T(8,128)S(1)} %get-tuple-element.45), channel_id=1, source_target_pairs={{0,1},{1,2},{2,3},{3,4},{4,5},{5,6},{6,7},{7,0},{8,9},{9,10},{10,1... | collective-permute-start | bytes 1572872 | tf_op jit(solution)/shard_map/ppermute | solution.py:295
  26.4 17.2 %collective-permute-start.3 = (f32[8,1,16,1024]{3,2,1,0:T(8,128)S(1)}, f32[8,1,16,1024]{3,2,1,0:T(8,128)S(1)}, u32[]{:S(2)}, u32[]{:S(2)}) collective-permute-start(f32[8,1,16,1024]{3,2,1,0:T(8,128)S(1)} %get-tuple-element.46), channel_id=1, source_target_pairs={{1,0},{2,1},{3,2},{4,3},{5,4},{6,5},{7,6},{0,7},{9,8},{10,9},{11,1... | collective-permute-start | bytes 1572872 | tf_op jit(solution)/shard_map/ppermute | solution.py:295
  35.2 17.5 %collective-permute-start.10 = (f32[8,1,16,1024]{3,2,1,0:T(8,128)S(1)}, f32[8,1,16,1024]{3,2,1,0:T(8,128)S(1)}, u32[]{:S(2)}, u32[]{:S(2)}) collective-permute-start(f32[8,1,16,1024]{3,2,1,0:T(8,128)S(1)} %get-tuple-element.57), channel_id=1, source_target_pairs={{0,1},{1,2},{2,3},{3,4},{4,5},{5,6},{6,7},{7,0},{8,9},{9,10},{10,1... | collective-permute-start | bytes 1572872 | tf_op jit(solution)/shard_map/ppermute | solution.py:295
  37.7 16.3 %collective-permute-start.11 = (f32[8,1,16,1024]{3,2,1,0:T(8,128)S(1)}, f32[8,1,16,1024]{3,2,1,0:T(8,128)S(1)}, u32[]{:S(2)}, u32[]{:S(2)}) collective-permute-start(f32[8,1,16,1024]{3,2,1,0:T(8,128)S(1)} %get-tuple-element.58), channel_id=1, source_target_pairs={{1,0},{2,1},{3,2},{4,3},{5,4},{6,5},{7,6},{0,7},{9,8},{10,9},{11,1... | collective-permute-start | bytes 1572872 | tf_op jit(solution)/shard_map/ppermute | solution.py:295
  47.3 17.8 %collective-permute-start.4 = (f32[8,1,16,1024]{3,2,1,0:T(8,128)}, f32[8,1,16,1024]{3,2,1,0:T(8,128)S(1)}, u32[]{:S(2)}, u32[]{:S(2)}) collective-permute-start(f32[8,1,16,1024]{3,2,1,0:T(8,128)} %get-tuple-element.48), channel_id=1, source_target_pairs={{0,1},{1,2},{2,3},{3,4},{4,5},{5,6},{6,7},{7,0},{8,9},{9,10},{10,1... | collective-permute-start | bytes 1572872 | tf_op jit(solution)/shard_map/ppermute | solution.py:295
  49.7 15.5 %collective-permute-start.5 = (f32[8,1,16,1024]{3,2,1,0:T(8,128)S(1)}, f32[8,1,16,1024]{3,2,1,0:T(8,128)S(1)}, u32[]{:S(2)}, u32[]{:S(2)}) collective-permute-start(f32[8,1,16,1024]{3,2,1,0:T(8,128)S(1)} %get-tuple-element.49), channel_id=1, source_target_pairs={{1,0},{2,1},{3,2},{4,3},{5,4},{6,5},{7,6},{0,7},{9,8},{10,9},{11,1... | collective-permute-start | bytes 1572872 | tf_op jit(solution)/shard_map/ppermute | solution.py:295
  57.8 17.9 %collective-permute-start.12 = (f32[8,1,16,1024]{3,2,1,0:T(8,128)}, f32[8,1,16,1024]{3,2,1,0:T(8,128)S(1)}, u32[]{:S(2)}, u32[]{:S(2)}) collective-permute-start(f32[8,1,16,1024]{3,2,1,0:T(8,128)} %get-tuple-element.60), channel_id=1, source_target_pairs={{0,1},{1,2},{2,3},{3,4},{4,5},{5,6},{6,7},{7,0},{8,9},{9,10},{10,1... | collective-permute-start | bytes 1572872 | tf_op jit(solution)/shard_map/ppermute | solution.py:295
  61.0 15.6 %collective-permute-start.13 = (f32[8,1,16,1024]{3,2,1,0:T(8,128)}, f32[8,1,16,1024]{3,2,1,0:T(8,128)S(1)}, u32[]{:S(2)}, u32[]{:S(2)}) collective-permute-start(f32[8,1,16,1024]{3,2,1,0:T(8,128)} %get-tuple-element.61), channel_id=1, source_target_pairs={{1,0},{2,1},{3,2},{4,3},{5,4},{6,5},{7,6},{0,7},{9,8},{10,9},{11,1... | collective-permute-start | bytes 1572872 | tf_op jit(solution)/shard_map/ppermute | solution.py:295
  65.2 31.2 %collective-permute-start.16 = (f32[2,8,1,8,512]{4,3,2,1,0:T(8,128)S(1)}, f32[2,8,1,8,512]{4,3,2,1,0:T(8,128)S(1)}, u32[]{:S(2)}, u32[]{:S(2)}) collective-permute-start(f32[2,8,1,8,512]{4,3,2,1,0:T(8,128)S(1)} %get-tuple-element.66), channel_id=1, source_target_pairs={{0,1},{1,2},{2,3},{3,4},{4,5},{5,6},{6,7},{7,0},{8,9},{9,10},{10,1... | collective-permute-start | bytes 786440 | tf_op jit(solution)/shard_map/ppermute | solution.py:295
  68.8 1.3 copy-start.5
  70.1 39.8 %collective-permute-start.6 = (f32[8,1,16,1024]{3,2,1,0:T(8,128)}, f32[8,1,16,1024]{3,2,1,0:T(8,128)S(1)}, u32[]{:S(2)}, u32[]{:S(2)}) collective-permute-start(f32[8,1,16,1024]{3,2,1,0:T(8,128)} %get-tuple-element.51), channel_id=1, source_target_pairs={{0,1},{1,2},{2,3},{3,4},{4,5},{5,6},{6,7},{7,0},{8,9},{9,10},{10,1... | collective-permute-start | bytes 1572872 | tf_op jit(solution)/shard_map/ppermute | solution.py:295
  73.3 36.6 %collective-permute-start.7 = (f32[8,1,16,1024]{3,2,1,0:T(8,128)}, f32[8,1,16,1024]{3,2,1,0:T(8,128)S(1)}, u32[]{:S(2)}, u32[]{:S(2)}) collective-permute-start(f32[8,1,16,1024]{3,2,1,0:T(8,128)} %get-tuple-element.52), channel_id=1, source_target_pairs={{1,0},{2,1},{3,2},{4,3},{5,4},{6,5},{7,6},{0,7},{9,8},{10,9},{11,1... | collective-permute-start | bytes 1572872 | tf_op jit(solution)/shard_map/ppermute | solution.py:295
  75.7 17.1 %collective-permute-start.18 = (f32[4,8,512]{2,1,0:T(8,128)S(1)}, f32[4,8,512]{2,1,0:T(8,128)S(1)}, u32[]{:S(2)}, u32[]{:S(2)}) collective-permute-start(f32[4,8,512]{2,1,0:T(8,128)S(1)} %shard_map.74.f), channel_id=1, source_target_pairs={{0,1},{1,2},{2,3},{3,4},{4,5},{5,6},{6,7},{7,0},{8,9},{9,10},{10,1... | collective-permute-start | bytes 196616 | tf_op jit(solution)/shard_map/ppermute | solution.py:295
  76.6 16.3 %collective-permute-start.19 = (f32[4,8,512]{2,1,0:T(8,128)S(1)}, f32[4,8,512]{2,1,0:T(8,128)S(1)}, u32[]{:S(2)}, u32[]{:S(2)}) collective-permute-start(f32[4,8,512]{2,1,0:T(8,128)S(1)} %shard_map.74.f), channel_id=1, source_target_pairs={{1,0},{2,1},{3,2},{4,3},{5,4},{6,5},{7,6},{0,7},{9,8},{10,9},{11,1... | collective-permute-start | bytes 196616 | tf_op jit(solution)/shard_map/ppermute | solution.py:295
  80.2 29.7 %copy-start.3 = (s32[4,16,1024]{2,1,0:T(8,128)S(1)}, s32[4,16,1024]{2,1,0:T(8,128)}, u32[]{:S(2)}) copy-start(s32[4,16,1024]{2,1,0:T(8,128)} %mask_ref.25) | copy-start | bytes 786436
  84.0 1.3 copy-start.7
  92.8 30.5 %collective-permute-start.14 = (f32[8,1,16,1024]{3,2,1,0:T(8,128)}, f32[8,1,16,1024]{3,2,1,0:T(8,128)}, u32[]{:S(2)}, u32[]{:S(2)}) collective-permute-start(f32[8,1,16,1024]{3,2,1,0:T(8,128)} %get-tuple-element.63), channel_id=1, source_target_pairs={{0,1},{1,2},{2,3},{3,4},{4,5},{5,6},{6,7},{7,0},{8,9},{9,10},{10,1... | collective-permute-start | bytes 1572872 | tf_op jit(solution)/shard_map/ppermute | solution.py:295
  92.8 30.5 %collective-permute-start.15 = (f32[8,1,16,1024]{3,2,1,0:T(8,128)}, f32[8,1,16,1024]{3,2,1,0:T(8,128)}, u32[]{:S(2)}, u32[]{:S(2)}) collective-permute-start(f32[8,1,16,1024]{3,2,1,0:T(8,128)} %get-tuple-element.64), channel_id=1, source_target_pairs={{1,0},{2,1},{3,2},{4,3},{5,4},{6,5},{7,6},{0,7},{9,8},{10,9},{11,1... | collective-permute-start | bytes 1572872 | tf_op jit(solution)/shard_map/ppermute | solution.py:295
  96.4 0.7 copy-start.9
  97.1 10.4 %collective-permute-start.17 = (f32[2,8,1,8,512]{4,3,2,1,0:T(8,128)}, f32[2,8,1,8,512]{4,3,2,1,0:T(8,128)}, u32[]{:S(2)}, u32[]{:S(2)}) collective-permute-start(f32[2,8,1,8,512]{4,3,2,1,0:T(8,128)} %get-tuple-element.68), channel_id=1, source_target_pairs={{1,0},{2,1},{3,2},{4,3},{5,4},{6,5},{7,6},{0,7},{9,8},{10,9},{11,1... | collective-permute-start | bytes 786440 | tf_op jit(solution)/shard_map/ppermute | solution.py:295
  107.5 0.9 copy-start.10
  109.9 1.6 copy-start.6
  115.3 8.1 %copy-start.8 = (f32[8,4,16,1024]{3,2,1,0:T(8,128)S(1)}, f32[8,4,16,1024]{3,2,1,0:T(8,128)}, u32[]{:S(2)}) copy-start(f32[8,4,16,1024]{3,2,1,0:T(8,128)} %copy-done.7) | copy-start | bytes 6291460
  119.2 12.1 %collective-permute-start.20 = (f32[8,1,8,512]{3,2,1,0:T(8,128)S(1)}, f32[8,1,8,512]{3,2,1,0:T(8,128)S(1)}, u32[]{:S(2)}, u32[]{:S(2)}) collective-permute-start(f32[8,1,8,512]{3,2,1,0:T(8,128)S(1)} %get-tuple-element.70), channel_id=1, source_target_pairs={{0,1},{1,2},{2,3},{3,4},{4,5},{5,6},{6,7},{7,0},{8,9},{9,10},{10,1... | collective-permute-start | bytes 393224 | tf_op jit(solution)/shard_map/ppermute | solution.py:295
  121.8 9.5 %collective-permute-start.21 = (f32[8,1,8,512]{3,2,1,0:T(8,128)S(1)}, f32[8,1,8,512]{3,2,1,0:T(8,128)S(1)}, u32[]{:S(2)}, u32[]{:S(2)}) collective-permute-start(f32[8,1,8,512]{3,2,1,0:T(8,128)S(1)} %get-tuple-element.72), channel_id=1, source_target_pairs={{1,0},{2,1},{3,2},{4,3},{5,4},{6,5},{7,6},{0,7},{9,8},{10,9},{11,1... | collective-permute-start | bytes 393224 | tf_op jit(solution)/shard_map/ppermute | solution.py:295
  133.3 2.0 %collective-permute-start.22 = (f32[8,2,8,512]{3,2,1,0:T(8,128)S(1)}, f32[8,2,8,512]{3,2,1,0:T(8,128)S(1)}, u32[]{:S(2)}, u32[]{:S(2)}) collective-permute-start(f32[8,2,8,512]{3,2,1,0:T(8,128)S(1)} %get-tuple-element.74), channel_id=1, source_target_pairs={{0,9},{1,10},{2,11},{3,12},{4,13},{5,14},{6,15},{7,8}} | collective-permute-start | bytes 786440 | tf_op jit(solution)/shard_map/ppermute | solution.py:376
  134.0 1.4 collective-permute-start.23
  134.7 0.7 collective-permute-start.24
  137.4 23.2 %collective-permute-start.25 = (f32[8,2,8,512]{3,2,1,0:T(8,128)S(1)}, f32[8,2,8,512]{3,2,1,0:T(8,128)S(1)}, u32[]{:S(2)}, u32[]{:S(2)}) collective-permute-start(f32[8,2,8,512]{3,2,1,0:T(8,128)S(1)} %get-tuple-element.75), channel_id=1, source_target_pairs={{8,17},{9,18},{10,19},{11,20},{12,21},{13,22},{14,23},{15,16}} | collective-permute-start | bytes 786440 | tf_op jit(solution)/shard_map/ppermute | solution.py:376
  138.7 35.7 %collective-permute-start.26 = (f32[8,2,8,512]{3,2,1,0:T(8,128)S(1)}, f32[8,2,8,512]{3,2,1,0:T(8,128)S(1)}, u32[]{:S(2)}, u32[]{:S(2)}) collective-permute-start(f32[8,2,8,512]{3,2,1,0:T(8,128)S(1)} %get-tuple-element.75), channel_id=1, source_target_pairs={{8,16},{9,17},{10,18},{11,19},{12,20},{13,21},{14,22},{15,23}} | collective-permute-start | bytes 786440 | tf_op jit(solution)/shard_map/ppermute | solution.py:376
  140.0 34.5 %collective-permute-start.27 = (f32[8,2,8,512]{3,2,1,0:T(8,128)S(1)}, f32[8,2,8,512]{3,2,1,0:T(8,128)S(1)}, u32[]{:S(2)}, u32[]{:S(2)}) collective-permute-start(f32[8,2,8,512]{3,2,1,0:T(8,128)S(1)} %get-tuple-element.75), channel_id=1, source_target_pairs={{8,23},{9,16},{10,17},{11,18},{12,19},{13,20},{14,21},{15,22}} | collective-permute-start | bytes 786440 | tf_op jit(solution)/shard_map/ppermute | solution.py:376
  174.5 18.4 %copy-start.1 = (f32[2,8,4,16,1024]{4,3,2,1,0:T(8,128)S(1)}, f32[2,8,4,16,1024]{4,3,2,1,0:T(8,128)}, u32[]{:S(2)}) copy-start(f32[2,8,4,16,1024]{4,3,2,1,0:T(8,128)} %starts_ref.9) | copy-start | bytes 12582916
  176.5 10.8 %collective-permute-start.28 = (f32[8,2,8,512]{3,2,1,0:T(8,128)S(1)}, f32[8,2,8,512]{3,2,1,0:T(8,128)S(1)}, u32[]{:S(2)}, u32[]{:S(2)}) collective-permute-start(f32[8,2,8,512]{3,2,1,0:T(8,128)S(1)} %get-tuple-element.76), channel_id=1, source_target_pairs={{16,25},{17,26},{18,27},{19,28},{20,29},{21,30},{22,31},{23,24}} | collective-permute-start | bytes 786440 | tf_op jit(solution)/shard_map/ppermute | solution.py:376
  177.8 13.0 %collective-permute-start.29 = (f32[8,2,8,512]{3,2,1,0:T(8,128)S(1)}, f32[8,2,8,512]{3,2,1,0:T(8,128)S(1)}, u32[]{:S(2)}, u32[]{:S(2)}) collective-permute-start(f32[8,2,8,512]{3,2,1,0:T(8,128)S(1)} %get-tuple-element.76), channel_id=1, source_target_pairs={{16,24},{17,25},{18,26},{19,27},{20,28},{21,29},{22,30},{23,31}} | collective-permute-start | bytes 786440 | tf_op jit(solution)/shard_map/ppermute | solution.py:376
  179.1 11.7 %collective-permute-start.30 = (f32[8,2,8,512]{3,2,1,0:T(8,128)S(1)}, f32[8,2,8,512]{3,2,1,0:T(8,128)S(1)}, u32[]{:S(2)}, u32[]{:S(2)}) collective-permute-start(f32[8,2,8,512]{3,2,1,0:T(8,128)S(1)} %get-tuple-element.76), channel_id=1, source_target_pairs={{16,31},{17,24},{18,25},{19,26},{20,27},{21,28},{22,29},{23,30}} | collective-permute-start | bytes 786440 | tf_op jit(solution)/shard_map/ppermute | solution.py:376
